TPU v7x, 32 devices: a whole 2x2x4 slice. The times are simulated.
32 devices in a mesh: dom: 8 (over y, x, core), blk: 4 (over z).
Axes of the slice: x: 2, y: 2, z: 4, core: 2. Of those that a mesh axis runs over, the one named last changes fastest.
Arguments:
- node_features: bfloat16 [8192, 512], P(('dom', 'blk')), may hold values from -6 to 6
- norm_gain: float32 [512], replicated, may hold values from 0.25 to 1.75
- w_query: bfloat16 [512, 512], replicated, may hold values from -0.25 to 0.25
- w_key: bfloat16 [512, 512], replicated, may hold values from -0.25 to 0.25
- w_value: bfloat16 [512, 512], replicated, may hold values from -0.25 to 0.25
- w_out: bfloat16 [512, 512], replicated, may hold values from -1.5 to 1.5
- w_message: bfloat16 [512, 512], replicated, may hold values from -1 to 1
- node_cluster: int32 [8192], P(('dom', 'blk')), may hold values from 0 to 15
- block_pattern: int32 [32, 4], P(('dom', 'blk')), may hold values from 0 to 1, as said below
- send_rows: int32 [256, 128], P(('dom', 'blk')), may hold values from 0 to 255
- send_counts: int32 [256], P(('dom', 'blk')), may hold values from 32 to 128, as said below
- edge_src: int32 [131072], P(('dom', 'blk')), may hold values from 0 to 1023
- edge_dst: int32 [131072], P(('dom', 'blk')), may hold values from 0 to 255
- out_grad: bfloat16 [8192, 512], P(('dom', 'blk')), may hold values from -6 to 6
Outputs:
- layer_out: bfloat16 [8192, 512], P(('dom', 'blk'))
- feature_grad: bfloat16 [8192, 512], P(('dom', 'blk'))
- weight_grads: float32 [5, 512, 512], replicated
- gain_grad: float32 [512], replicated
Inputs may be any that keep to these rules, and one draw needn't show every extreme that they name: `block_pattern`: row g has a 1 at column (g mod 4); other entries are 0 or 1. `send_counts`: entry g * 8 + p is how many leading slots of device g's block to dom peer p are live; every device has one peer whose block has all 128 slots live.
All inputs are finite; a program needn't handle non-finite values.
Results may differ from a plain program's by a relative error of at most 0.013.
Values may be sent and summed in bfloat16 or wider, within the bound.
A program may use at most 128 MiB of HBM per device.

v0:
```python
from functools import partial

import jax
import jax.numpy as jnp
from jax import lax
from jax.sharding import PartitionSpec as P

HEADS = 8
HEAD_DIM = 64


epsilon = 1e-06
score_shift = 8.0


def settle(array):
    return lax.optimization_barrier(array.astype(jnp.bfloat16)).astype(jnp.float32)


def rms_norm(features, norm_gain):
    scaling = lax.rsqrt(jnp.mean(features * features, axis=-1, keepdims=True) + epsilon)
    return features * scaling * norm_gain


def head_norm(projected):
    head_view = projected.reshape(projected.shape[0], HEADS, HEAD_DIM)
    scaling = lax.rsqrt(jnp.mean(head_view * head_view, axis=-1, keepdims=True) + epsilon)
    return (head_view * scaling).reshape(projected.shape)


def block_weights(query_heads, key_heads, allowed):
    scaling = score_shift / HEAD_DIM
    scores = (
        jnp.einsum("rhe,khe->hrk", query_heads, key_heads, preferred_element_type=jnp.float32)
        * scaling
    )
    return jnp.where(allowed[None], jnp.exp(scores - score_shift), 0.0)


def attend_piece(running, shard_piece, offset, query_heads, query_labels, pattern_row, skip_empty):
    key_rows, value_rows, key_labels = shard_piece
    row_count = query_heads.shape[0]
    piece_rows = key_rows.shape[0]
    part_count = max(piece_rows // row_count, 1)
    block_index = jnp.arange(pattern_row.shape[0], dtype=jnp.int32)
    for position in range(part_count):
        first_row = position * piece_rows // part_count
        last_row = (position + 1) * piece_rows // part_count
        part_rows = last_row - first_row
        key_part = key_rows[first_row:last_row].reshape(part_rows, HEADS, HEAD_DIM)
        value_part = value_rows[first_row:last_row].reshape(part_rows, HEADS, HEAD_DIM)
        label_part = key_labels[first_row:last_row]
        owners = (offset + first_row + jnp.arange(part_rows, dtype=jnp.int32)) // row_count
        block_flags = jnp.sum(
            jnp.where(owners[:, None] == block_index[None, :], pattern_row[None, :], 0), axis=1
        )
        allowed = (query_labels[:, None] == label_part[None, :]) & (block_flags[None, :] == 1)

        def accumulate(current, key_part=key_part, value_part=value_part, allowed=allowed):
            numer, denom = current
            weights = block_weights(query_heads, key_part, allowed)
            denom = denom + jnp.sum(weights, axis=2).T
            numer = numer + jnp.einsum(
                "hrk,khe->rhe",
                weights.astype(jnp.bfloat16),
                value_part,
                preferred_element_type=jnp.float32,
            )
            return (numer, denom)

        running = accumulate(running)
    return running


def pair_gradients(query_heads, grad_heads, correction, key_part, value_part, allowed):
    scaling = score_shift / HEAD_DIM
    weights = block_weights(query_heads, key_part, allowed)
    grad_dots = jnp.einsum(
        "rhe,khe->hrk", grad_heads, value_part, preferred_element_type=jnp.float32
    )
    slopes = (weights * (grad_dots - correction.T[:, :, None])).astype(jnp.bfloat16)
    dq_part = (
        jnp.einsum("hrk,khe->rhe", slopes, key_part, preferred_element_type=jnp.float32) * scaling
    )
    dk_part = (
        jnp.einsum("hrk,rhe->khe", slopes, query_heads, preferred_element_type=jnp.float32)
        * scaling
    )
    dv_part = jnp.einsum(
        "hrk,rhe->khe", weights.astype(jnp.bfloat16), grad_heads, preferred_element_type=jnp.float32
    )
    return (dq_part, dk_part, dv_part)


def key_block(
    query_heads, grad_heads, correction, query_labels, skip_empty, dq_total, block_inputs
):
    key_part, value_part, label_part, block_flag = block_inputs
    row_count = query_heads.shape[0]
    allowed = (query_labels[:, None] == label_part[None, :]) & (block_flag == 1)
    dq_part, dk_part, dv_part = pair_gradients(
        query_heads, grad_heads, correction, key_part, value_part, allowed
    )
    flat_terms = (dk_part.reshape(row_count, -1), dv_part.reshape(row_count, -1))
    return (dq_total + settle(dq_part), flat_terms)


def local(
    node_features,
    norm_gain,
    w_query,
    w_key,
    w_value,
    w_out,
    w_message,
    node_cluster,
    block_pattern,
    send_rows,
    send_counts,
    edge_src,
    edge_dst,
    out_grad,
):
    row_count = node_features.shape[0]
    feat_width = node_features.shape[1]
    peer_count = lax.axis_size("dom")
    block_count = lax.axis_size("blk")
    slot_count = send_rows.shape[1]
    features = node_features.astype(jnp.float32)
    normed_f, norm_pull = jax.vjp(rms_norm, features, norm_gain)
    normed = normed_f.astype(jnp.bfloat16)
    live_slots = jnp.arange(slot_count, dtype=jnp.int32)[None, :] < send_counts[:, None]
    outgoing = jnp.where(live_slots[:, :, None], normed[send_rows], jnp.zeros((), jnp.bfloat16))
    incoming = lax.all_to_all(outgoing, "dom", split_axis=0, concat_axis=0, tiled=True)
    query_f, query_pull = jax.vjp(
        head_norm, jnp.dot(normed, w_query, preferred_element_type=jnp.float32)
    )
    key_f, key_pull = jax.vjp(head_norm, jnp.dot(normed, w_key, preferred_element_type=jnp.float32))
    queries = query_f.astype(jnp.bfloat16)
    key_flat = key_f.astype(jnp.bfloat16)
    value_flat = jnp.dot(normed, w_value, preferred_element_type=jnp.float32).astype(jnp.bfloat16)
    query_heads = queries.reshape(row_count, HEADS, HEAD_DIM)
    pattern_row = block_pattern[0]
    start_state = (
        jnp.zeros((row_count, HEADS, HEAD_DIM), jnp.float32),
        jnp.zeros((row_count, HEADS), jnp.float32),
    )
    fold_step = partial(
        attend_piece,
        query_heads=query_heads,
        query_labels=node_cluster,
        pattern_row=pattern_row,
        skip_empty=False,
    )
    key_set = None
    key_set = (
        lax.all_gather(key_flat, "blk", axis=0, tiled=True),
        lax.all_gather(value_flat, "blk", axis=0, tiled=True),
        lax.all_gather(node_cluster, "blk", axis=0, tiled=True),
    )
    numer, denom = fold_step(start_state, key_set, 0)
    slot_table = incoming.reshape(peer_count * slot_count, feat_width)
    pair_index = edge_src * row_count + edge_dst
    edge_counts = jnp.zeros((peer_count * slot_count * row_count,), jnp.int32).at[pair_index].add(1)
    edge_counts = edge_counts.reshape(peer_count * slot_count, row_count).astype(jnp.bfloat16)
    degree = jnp.maximum(
        jax.ops.segment_sum(jnp.ones(edge_dst.shape, jnp.float32), edge_dst, row_count), 1.0
    )
    neighbour_sum = jnp.einsum(
        "sr,sd->rd", edge_counts, slot_table, preferred_element_type=jnp.float32
    )
    mean_rows = (neighbour_sum / degree[:, None]).astype(jnp.bfloat16)
    local_term = jnp.dot(mean_rows, w_message, preferred_element_type=jnp.float32)
    attn_heads = (numer / denom[..., None]).astype(jnp.bfloat16)
    attn_rows = attn_heads.reshape(row_count, feat_width)
    attn_proj = jnp.dot(attn_rows, w_out, preferred_element_type=jnp.float32)
    layer_out = (features + local_term + attn_proj).astype(jnp.bfloat16)
    grad_attn = jnp.einsum(
        "rd,ed->re", out_grad, w_out, preferred_element_type=jnp.float32
    ).reshape(row_count, HEADS, HEAD_DIM)
    grad_heads = (grad_attn / denom[..., None]).astype(jnp.bfloat16)
    correction = jnp.sum(grad_attn * attn_heads.astype(jnp.float32), axis=-1) / denom
    key_rows, value_rows, key_labels = key_set
    block_inputs = (
        key_rows.reshape(block_count, row_count, HEADS, HEAD_DIM),
        value_rows.reshape(block_count, row_count, HEADS, HEAD_DIM),
        key_labels.reshape(block_count, row_count),
        pattern_row,
    )
    block_step = partial(key_block, query_heads, grad_heads, correction, node_cluster, False)
    dq_heads, (key_terms, value_terms) = lax.scan(
        block_step, jnp.zeros((row_count, HEADS, HEAD_DIM), jnp.float32), block_inputs
    )
    key_grad, value_grad = (
        lax.psum_scatter(
            key_terms.reshape(block_count * row_count, feat_width).astype(jnp.bfloat16),
            "blk",
            scatter_dimension=0,
            tiled=True,
        ).astype(jnp.float32),
        lax.psum_scatter(
            value_terms.reshape(block_count * row_count, feat_width).astype(jnp.bfloat16),
            "blk",
            scatter_dimension=0,
            tiled=True,
        ).astype(jnp.float32),
    )
    dq_flat = dq_heads.reshape(row_count, feat_width)
    dquery = query_pull(dq_flat)[0].astype(jnp.bfloat16)
    dkey = key_pull(key_grad)[0].astype(jnp.bfloat16)
    dvalue = value_grad.astype(jnp.bfloat16)
    dmessage = (
        jnp.einsum("rd,ed->re", out_grad, w_message, preferred_element_type=jnp.float32)
        / degree[:, None]
    ).astype(jnp.bfloat16)
    slot_grads = jnp.dot(edge_counts, dmessage, preferred_element_type=jnp.float32).astype(
        jnp.bfloat16
    )
    returned = lax.all_to_all(
        slot_grads.reshape(peer_count, slot_count, feat_width),
        "dom",
        split_axis=0,
        concat_axis=0,
        tiled=True,
    )
    returned = jnp.where(live_slots[:, :, None], returned.astype(jnp.float32), 0.0)
    halo_grad = jax.ops.segment_sum(
        returned.reshape(peer_count * slot_count, feat_width), send_rows.reshape(-1), row_count
    )
    dnormed = jnp.einsum("rd,ed->re", dquery, w_query, preferred_element_type=jnp.float32)
    dnormed = dnormed + jnp.einsum("rd,ed->re", dkey, w_key, preferred_element_type=jnp.float32)
    dnormed = dnormed + jnp.einsum("rd,ed->re", dvalue, w_value, preferred_element_type=jnp.float32)
    dnormed = dnormed + halo_grad
    dfeatures, gain_term = norm_pull(dnormed)
    feature_grad = (out_grad.astype(jnp.float32) + dfeatures).astype(jnp.bfloat16)
    weight_terms = jnp.stack(
        [
            jnp.einsum("rd,re->de", normed, dquery, preferred_element_type=jnp.float32),
            jnp.einsum("rd,re->de", normed, dkey, preferred_element_type=jnp.float32),
            jnp.einsum("rd,re->de", normed, dvalue, preferred_element_type=jnp.float32),
            jnp.einsum("rd,re->de", attn_rows, out_grad, preferred_element_type=jnp.float32),
            jnp.einsum("rd,re->de", mean_rows, out_grad, preferred_element_type=jnp.float32),
        ]
    )
    weight_sums, gain_sum = lax.psum((weight_terms, gain_term), ("dom", "blk"))
    return (layer_out, feature_grad, weight_sums, gain_sum)


def solution(mesh):
    placed = (
        P(("dom", "blk"), None),
        P(),
        P(),
        P(),
        P(),
        P(),
        P(),
        P(("dom", "blk")),
        P(("dom", "blk"), None),
        P(("dom", "blk"), None),
        P(("dom", "blk")),
        P(("dom", "blk")),
        P(("dom", "blk")),
        P(("dom", "blk"), None),
    )
    return jax.shard_map(
        local,
        mesh=mesh,
        in_specs=placed,
        out_specs=(P(("dom", "blk"), None), P(("dom", "blk"), None), P(), P()),
        check_vma=False,
    )
```

profile of v0, /device:TPU:0, one launch (start us, length us, event | category | flops | bytes accessed | tf_op | source)
XLA Modules:
  0.0 394.7 jit_solution(18400404368200402378)
XLA Ops:
  9.5 1.3 fusion.53
  16.5 12.6 %all-gather = s32[4,1,256]{2,1,0:T(1,128)S(1)} all-gather(s32[1,1,256]{2,1,0:T(1,128)S(1)} %bitcast.217), channel_id=1, replica_groups=mesh['dom'=8,'blk'=4] {'blk'}, dimensions={0}, use_global_device_ids=true | all-gather | bytes 5120 | tf_op jit(solution)/shard_map/all_gather | solution.py:159
  30.6 12.5 %all-gather.6.cloned.1.call-done = bf16[1024,512]{1,0:T(8,128)(2,1)} async-done(((bf16[256,512]{1,0:T(8,128)(2,1)}), bf16[1024,512]{1,0:T(8,128)(2,1)}) %all-gather.6.cloned.1.call-update) | async-done | bytes 1048592 | tf_op jit(solution)/shard_map/all_gather | solution.py:157
  43.1 1.3 fusion.50
  47.8 24.3 %all-gather.4.cloned.1.call-done = bf16[1024,512]{1,0:T(8,128)(2,1)} async-done(((bf16[256,512]{1,0:T(8,128)(2,1)}), bf16[1024,512]{1,0:T(8,128)(2,1)}) %all-gather.4.cloned.1.call-update) | async-done | bytes 1048592 | tf_op jit(solution)/shard_map/all_gather | solution.py:158
  72.1 2.2 fusion.51
  74.3 1.8 copy.110
  76.1 1.8 copy.118
  77.9 1.8 copy.121
  79.6 1.8 copy.124
  81.4 2.1 reshape.506
  83.5 3.1 copy.130
  86.6 2.1 reshape.507
  88.7 3.0 copy.131
  98.1 39.7 %while.17 = (s32[]{:T(128)}, f32[256,8,64]{0,2,1:T(8,128)S(1)}, bf16[4,256,512]{1,2,0:T(8,128)(2,1)}, bf16[4,256,512]{2,1,0:T(8,128)(2,1)}, bf16[4,256,8,64]{1,3...) while((s32[]{:T(128)}, f32[256,8,64]{0,2,1:T(8,128)S(1)}, ...), condition=%wide.region_15.16_spmd.clone, body=%wide.region_14.15_spmd.clone.sunk | while | flops 340262912 | bytes 31863044 | solution.py:191
  99.5 1.6 bitcast_select_fusion.2
  101.1 1.3 copy-done.1
  102.4 1.4 fusion.139
  109.4 1.6 bitcast_select_fusion.2
  111.0 1.3 copy-done.1
  112.3 1.4 fusion.139
  119.3 1.6 bitcast_select_fusion.2
  120.9 1.3 copy-done.1
  122.2 1.4 fusion.139
  129.2 1.6 bitcast_select_fusion.2
  130.8 1.3 copy-done.1
  132.1 1.4 fusion.139
  137.8 2.3 copy.132
  140.1 4.0 %gather_fusion = bf16[1024,512]{1,0:T(8,128)(2,1)S(1)} fusion(bf16[256,512]{1,0:T(8,128)(2,1)S(1)} %fusion.32, s32[1024]{0:T(1024)S(1)} %fusion.46), kind=kCustom, calls=%fused_computation | custom fusion | bytes 2101248 | tf_op jit(solution)/shard_map/gather | solution.py:133
  145.4 4.2 %all-to-all-start = ((bf16[8,128,512]{2,1,0:T(8,128)(2,1)}), bf16[8,128,512]{2,1,0:T(8,128)(2,1)}, u32[]{:S(2)}, u32[]{:S(2)}) async-start(bf16[8,128,512]{2,1,0:T(8,128)(2,1)} %broadcast_select_fusion), calls=%async_computation | async-start | bytes 2097152 | tf_op jit(solution)/shard_map/all_to_all | solution.py:134
  149.7 22.3 %scatter_custom_fusion = s32[262144]{0:T(1024)S(1)} fusion(s32[4096]{0:T(1024)S(1)} %compare_select_fusion, s32[4096]{0:T(1024)S(1)} %broadcast.456, s32[]{:T(128)} %constant.112.clone.1), kind=kCustom, calls=%fused_computation.92 | custom fusion | flops 4096 | bytes 1048580 | tf_op jit(solution)/shard_map/scatter-add | solution.py:164
  172.3 28.8 %scatter_custom_fusion.1 = f32[256]{0:T(256)S(1)} fusion(s32[4096]{0:T(1024)S(1)} %copy-done.44, f32[4096]{0:T(1024)S(1)} %broadcast.457, f32[]{:T(128)} %constant.116.clone.1), kind=kCustom, calls=%fused_computation.144 | custom fusion | flops 4096 | bytes 1028 | tf_op jit(solution)/shard_map/scatter-add | solution.py:167
  201.1 1.7 convolution_convert_fusion
  202.9 4.3 %all-to-all-start.1 = ((bf16[8,128,512]{2,1,0:T(8,128)(2,1)}), bf16[8,128,512]{2,1,0:T(8,128)(2,1)}, u32[]{:S(2)}, u32[]{:S(2)}) async-start(bf16[8,128,512]{2,1,0:T(8,128)(2,1)} %bitcast.32), calls=%async_computation.3 | async-start | bytes 2097152 | tf_op jit(solution)/shard_map/all_to_all | solution.py:219
  207.2 2.4 fusion.21
  209.9 1.3 fusion.18
  213.7 1.3 fusion.17
  215.0 15.1 %reduce-scatter.5.cloned.1.call-done = bf16[256,512]{1,0:T(8,128)(2,1)} async-done(((bf16[1024,512]{1,0:T(8,128)(2,1)}), bf16[256,512]{1,0:T(8,128)(2,1)}) %reduce-scatter.5.cloned.1.call-update) | async-done | bytes 262160 | tf_op jit(solution)/shard_map/reduce_scatter | solution.py:201
  230.1 2.2 fusion.16
  232.3 1.3 fusion.15
  233.6 1.3 fusion.14
  236.9 1.6 convert_select_fusion
  238.6 1.5 fusion.60
  241.9 6.8 %scatter_fusion = f32[256,512]{1,0:T(8,128)S(1)} fusion(f32[256,512]{1,0:T(8,128)S(1)} %convolution_add_fusion.3, s32[1024]{0:T(1024)S(1)} %bitcast.219, f32[1024,512]{1,0:T(8,128)S(1)} %bitcast.195), kind=kCustom, calls=%fused_computation.3 | custom fusion | flops 524288 | bytes 6295552 | tf_op jit(solution)/shard_map/scatter-add | solution.py:227
  248.9 38.9 %psum.15 = f32[512]{0:T(512)} all-reduce(f32[512]{0:T(512)S(1)} %get-tuple-element.245), channel_id=1, replica_groups=mesh['dom'=8,'blk'=4] {'dom','blk'}, use_global_device_ids=true, to_apply=%region_24.25 | all-reduce | flops 512 | bytes 4096 | tf_op jit(solution)/shard_map/psum | solution.py:245
  287.8 1.9 fusion.37
  289.7 92.6 %all-reduce.2.cloned.1.call-done = f32[5,512,512]{2,1,0:T(8,128)} async-done(((f32[5,512,512]{2,1,0:T(8,128)}), f32[5,512,512]{2,1,0:T(8,128)}) %all-reduce.2.cloned.1.call-update) | async-done | bytes 5242896 | tf_op jit(solution)/shard_map/psum | solution.py:245
  382.4 5.8 %copy.188 = f32[5,512,512]{2,1,0:T(8,128)} copy(f32[5,512,512]{2,1,0:T(8,128)} %all-reduce.2.cloned.1.call-done) | data formatting | bytes 10485760
  (227 shorter events, 46.4 us)
Async XLA Ops:
  7.2 193.9 %copy-start = (bf16[512,512]{1,0:T(8,128)(2,1)S(1)}, bf16[512,512]{1,0:T(8,128)(2,1)}, u32[]{:S(2)}) copy-start(bf16[512,512]{1,0:T(8,128)(2,1)} %param.22) | copy-start | bytes 1572868
  7.2 35.9 %all-gather.6.cloned.1.call-start = ((), (), s32[]{:S(2)}) async-start(), calls=%async_computation.5 | async-start | bytes 1310720 | tf_op jit(solution)/shard_map/all_gather | solution.py:157
  10.8 1.5 copy-start.3
  11.0 1.3 copy-start.21
  11.1 2.3 copy-start.23
  11.4 2.1 copy-start.8
  12.3 59.8 %all-gather.4.cloned.1.call-start = ((), (), s32[]{:S(2)}) async-start(), calls=%async_computation.4 | async-start | bytes 1310720 | tf_op jit(solution)/shard_map/all_gather | solution.py:158
  13.4 197.8 %reduce-scatter.3.cloned.1.call-start = ((), (), s32[]{:S(2)}) async-start(), calls=%async_computation.6 | async-start | bytes 1310720 | tf_op jit(solution)/shard_map/reduce_scatter | solution.py:195
  14.0 2.3 copy-start.5
  14.0 2.5 copy-start.40
  14.0 15.1 %copy-start.45 = (s32[1,4]{1,0:T(1,128)S(1)}, s32[1,4]{1,0:T(1,128)}, u32[]{:S(2)}) copy-start(s32[1,4]{1,0:T(1,128)} %param.24) | copy-start | bytes 52
  14.0 16.2 %copy-start.12 = (bf16[256,512]{1,0:T(8,128)(2,1)S(1)}, bf16[256,512]{1,0:T(8,128)(2,1)}, u32[]{:S(2)}) copy-start(bf16[256,512]{1,0:T(8,128)(2,1)} %param.29) | copy-start | bytes 786436
  14.0 16.2 %copy-start.19 = (bf16[512,512]{1,0:T(8,128)(2,1)S(1)}, bf16[512,512]{1,0:T(8,128)(2,1)}, u32[]{:S(2)}) copy-start(bf16[512,512]{1,0:T(8,128)(2,1)} %param.21) | copy-start | bytes 1572868
  47.8 33.7 %copy-start.10 = (bf16[1024,512]{1,0:T(8,128)(2,1)S(1)}, bf16[1024,512]{1,0:T(8,128)(2,1)}, u32[]{:S(2)}) copy-start(bf16[1024,512]{1,0:T(8,128)(2,1)} %all-gather.6.cloned.1.call-done) | copy-start | bytes 3145732
  83.5 3.1 copy-start.11
  88.7 3.1 copy-start.36
  88.7 3.1 copy-start.39
  105.1 1.6 copy-start.2
  111.0 1.3 copy-start.1
  115.0 1.6 copy-start.2
  120.9 1.3 copy-start.1
  124.9 1.6 copy-start.2
  130.8 1.3 copy-start.1
  134.8 1.6 copy-start.2
  137.8 2.3 copy-start.42
  140.1 4.0 %copy-start.46 = (s32[8]{0:T(128)S(1)}, s32[8]{0:T(128)}, u32[]{:S(2)}) copy-start(s32[8]{0:T(128)} %param.26) | copy-start | bytes 100
  144.2 5.5 %copy-start.43 = (s32[4096]{0:T(1024)S(1)}, s32[4096]{0:T(1024)}, u32[]{:S(2)}) copy-start(s32[4096]{0:T(1024)} %param.27) | copy-start | bytes 49156
  144.2 5.5 %copy-start.44 = (s32[4096]{0:T(1024)S(1)}, s32[4096]{0:T(1024)}, u32[]{:S(2)}) copy-start(s32[4096]{0:T(1024)} %param.28) | copy-start | bytes 49156
  145.4 57.5 %all-to-all-start = ((bf16[8,128,512]{2,1,0:T(8,128)(2,1)}), bf16[8,128,512]{2,1,0:T(8,128)(2,1)}, u32[]{:S(2)}, u32[]{:S(2)}) async-start(bf16[8,128,512]{2,1,0:T(8,128)(2,1)} %broadcast_select_fusion), calls=%async_computation | async-start | bytes 2097152 | tf_op jit(solution)/shard_map/all_to_all | solution.py:134
  149.6 80.4 %reduce-scatter.5.cloned.1.call-start = ((), (), s32[]{:S(2)}) async-start(), calls=%async_computation.7 | async-start | bytes 1310720 | tf_op jit(solution)/shard_map/reduce_scatter | solution.py:201
  202.9 34.0 %all-to-all-start.1 = ((bf16[8,128,512]{2,1,0:T(8,128)(2,1)}), bf16[8,128,512]{2,1,0:T(8,128)(2,1)}, u32[]{:S(2)}, u32[]{:S(2)}) async-start(bf16[8,128,512]{2,1,0:T(8,128)(2,1)} %bitcast.32), calls=%async_computation.3 | async-start | bytes 2097152 | tf_op jit(solution)/shard_map/all_to_all | solution.py:219
  207.1 2.5 copy-start.6
  207.2 175.2 %all-reduce.2.cloned.1.call-start = ((), (), s32[]{:S(2)}) async-start(), calls=%async_computation.8 | async-start | bytes 10485760 | tf_op jit(solution)/shard_map/psum | solution.py:245
  209.6 1.5 copy-start.4
  209.8 2.7 copy-start.13
  211.2 1.6 copy-start.9
  213.6 19.9 %copy-start.15 = (bf16[256,512]{1,0:T(8,128)(2,1)}, bf16[256,512]{1,0:T(8,128)(2,1)S(1)}, u32[]{:S(2)}) copy-start(bf16[256,512]{1,0:T(8,128)(2,1)S(1)} %fusion.35) | copy-start | bytes 786436
  213.6 18.7 %copy-start.28 = (bf16[256,8,64]{0,2,1:T(8,128)(2,1)S(1)}, bf16[256,8,64]{0,2,1:T(8,128)(2,1)}, u32[]{:S(2)}) copy-start(bf16[256,8,64]{0,2,1:T(8,128)(2,1)} %get-tuple-element.302) | copy-start | bytes 786436
  213.6 19.9 %copy-start.31 = (bf16[256,512]{1,0:T(8,128)(2,1)S(1)}, bf16[256,512]{1,0:T(8,128)(2,1)}, u32[]{:S(2)}) copy-start(bf16[256,512]{1,0:T(8,128)(2,1)} %fusion.21) | copy-start | bytes 786436
  235.8 2.7 copy-start.14
  236.9 3.2 copy-start.18
  236.9 3.2 copy-start.20
  236.9 3.2 copy-start.29
  238.5 2.6 copy-start.16
  238.6 2.6 copy-start.17
  238.6 2.9 copy-start.22
  238.6 2.9 copy-start.27
  241.9 6.8 %copy-start.41 = (f32[512]{0:T(512)S(1)}, f32[512]{0:T(512)}, u32[]{:S(2)}) copy-start(f32[512]{0:T(512)} %param.17) | copy-start | bytes 6148
  (12 other events, 12.2 us)
Sparse Core Ops, SparseCore 0:
  12.4 30.6 all-gather.5
  44.7 27.3 all-gather.3
  140.2 26.6 reduce-scatter.2
  203.0 27.0 reduce-scatter.4
  236.1 146.2 all-reduce.1
where the time goes:
time: 396 us; the launch traced here: 395 us
  waiting for transfers between devices  145 us (37%)
  other arithmetic  70.1 us (18%)
  local copies, waits for them, and re-layouts  57.7 us (15%)
  blocking collectives  51.6 us (13%)
  matrix products  44.4 us (11%)
  between operations  14.7 us (4%)
  starting transfers between devices  8.7 us (2%)
    psum x1, waiting for transfers between devices, local(): weight_sums, gain_sum = lax.psum((weight_terms, gain_term), ('dom', 'blk'))  92.6 us
    psum x1, blocking collectives, local(): weight_sums, gain_sum = lax.psum((weight_terms, gain_term), ('dom', 'blk'))  38.9 us
    scatter-add x1, other arithmetic, local(): jax.ops.segment_sum(jnp.ones(edge_dst.shape, jnp.float32), edge_dst, row_...  28.8 us
    all_gather x1, waiting for transfers between devices, local(): lax.all_gather(value_flat, 'blk', axis=0, tiled=True)  24.3 us
    scatter-add x1, other arithmetic, local(): jnp.zeros((peer_count * slot_count * row_count,), jnp.int32).at[pair_index]  22.3 us
    reduce_scatter x1, waiting for transfers between devices, local(): lax.psum_scatter(value_terms.reshape(block_count * row_count, feat_width)...  15.1 us
    unnamed x94, local copies, waits for them, and re-layouts  14.9 us
    all_gather x1, blocking collectives, local(): lax.all_gather(node_cluster, 'blk', axis=0, tiled=True)  12.6 us
  transfers between devices with their start and end apart: 7, of which 4 were waited for; matrix products, arithmetic and copies ran while one was open for 24% of the time, Pallas kernels for 0%

commit v1 on v0

v1 whole, which is shorter than its diff:
```python
from functools import partial

import jax
import jax.numpy as jnp
from jax import lax
from jax.experimental import pallas as pl
from jax.experimental.pallas import tpu as pltpu
from jax.sharding import PartitionSpec as P

HEADS = 8
HEAD_DIM = 64
SCALE = 8.0 / HEAD_DIM
SHIFT = 8.0
EPS = 1e-06
MASKED = -1e30
EDGE_PART = 512
MESH = pl.DeviceIdType.MESH
F32 = jnp.float32
BF16 = jnp.bfloat16


def params(collective_id=None):
    return pltpu.CompilerParams(
        vmem_limit_bytes=56 * 1024 * 1024,
        collective_id=collective_id,
        has_side_effects=collective_id is not None,
    )


def mul(a, b, ca, cb):
    return lax.dot_general(a, b, (((ca,), (cb,)), ((), ())), preferred_element_type=F32)


def row_scale(x):
    return lax.rsqrt(jnp.mean(x * x, axis=-1, keepdims=True) + EPS)


def head_norm(x):
    view = x.reshape(HEADS, HEAD_DIM, x.shape[1])
    scaling = lax.rsqrt(jnp.mean(view * view, axis=1, keepdims=True) + EPS)
    return view * scaling, scaling


def head_norm_pull(y, scaling, dy):
    dy = dy.reshape(y.shape)
    dx = scaling * (dy - y * jnp.mean(y * dy, axis=1, keepdims=True))
    return dx.reshape(-1, y.shape[2])


def remote(src, dst, send, recv, axis, peer):
    return pltpu.make_async_remote_copy(
        src_ref=src, dst_ref=dst, send_sem=send, recv_sem=recv,
        device_id={axis: peer}, device_id_type=MESH,
    )


def exchange_kernel(
    nd, nb,
    feat, gout, gain, wm, meta, sidx, esrc, edst,
    feats, gouts, metas, mean_out, halo_out,
    sbuf, rbuf, sback, rback, cnt, onehot,
    own_sem, zsend, zrecv, asend, arecv, bsend, brecv,
):
    me = lax.axis_index("blk")
    my_dom = lax.axis_index("dom")
    rows = feat.shape[0]
    cap = sidx.shape[1]
    barrier = pltpu.get_barrier_semaphore()
    for k in range(1, nd):
        pl.semaphore_signal(
            barrier, inc=1, device_id={"dom": lax.rem(my_dom + k, nd)}, device_id_type=MESH
        )
    for k in range(1, nb):
        pl.semaphore_signal(
            barrier, inc=1, device_id={"blk": lax.rem(me + k, nb)}, device_id_type=MESH
        )
    pl.semaphore_wait(barrier, nd - 1 + nb - 1)

    own = ((feat, feats), (gout, gouts), (meta, metas))
    local = [pltpu.make_async_copy(s, d.at[me], own_sem.at[k]) for k, (s, d) in enumerate(own)]
    for c in local:
        c.start()

    def line_copy(step, way, k, block):
        src, dst = own[k]
        if step > 0:
            src = dst.at[block]
        peer = me + 1 if way == 0 else me - 1
        return remote(
            src, dst.at[block], zsend.at[way, step, k], zrecv.at[way, step, k], "blk", peer
        )

    def line_send(step, start):
        for way in range(2):
            sends = (me + 1 < nb) & (me - step >= 0) if way == 0 else (me >= 1) & (me + step < nb)
            block = me - step if way == 0 else me + step

            @pl.when(sends)
            def _():
                for k in range(3):
                    c = line_copy(step, way, k, block)
                    if start:
                        c.start()
                    else:
                        c.wait_send()

    def line_recv(step):
        for way in range(2):
            block = me - 1 - step if way == 0 else me + 1 + step
            got = block >= 0 if way == 0 else block < nb

            @pl.when(got)
            def _():
                for k in range(3):
                    line_copy(step, way, k, block).wait_recv()

    line_send(0, True)

    x = feat[...].astype(F32)
    normed = (x * row_scale(x) * gain[...]).astype(BF16)
    row_ids = lax.broadcasted_iota(jnp.int32, (rows, cap), 0)

    def swap(src, dst, send, recv, k, incoming):
        to = lax.rem(my_dom + k, nd)
        origin = lax.rem(my_dom + nd - k, nd)
        return remote(
            src.at[to], dst.at[origin if incoming else my_dom], send.at[k], recv.at[k], "dom", to
        )

    for p in range(nd):
        hot = jnp.where(row_ids == sidx[p : p + 1, :], 1.0, 0.0).astype(BF16)
        onehot[:, p * cap : (p + 1) * cap] = hot
        sbuf[p] = mul(hot, normed, 0, 0).astype(BF16)
    for k in range(1, nd):
        swap(sbuf, rbuf, asend, arecv, k, False).start()
    rbuf[my_dom] = sbuf[my_dom]

    slot_ids = lax.broadcasted_iota(jnp.int32, (nd * cap, EDGE_PART), 0)
    dst_ids = lax.broadcasted_iota(jnp.int32, (rows, EDGE_PART), 0)
    cnt[...] = jnp.zeros_like(cnt)

    def count(c, carry):
        hot_src = jnp.where(slot_ids == esrc[pl.ds(c, 1), :], 1.0, 0.0).astype(BF16)
        hot_dst = jnp.where(dst_ids == edst[pl.ds(c, 1), :], 1.0, 0.0).astype(BF16)
        cnt[...] += mul(hot_dst, hot_src, 1, 1)
        return carry

    lax.fori_loop(0, esrc.shape[0], count, 0)
    counts = cnt[...]
    degree = jnp.maximum(jnp.sum(counts, axis=1, keepdims=True), 1.0)
    counts = counts.astype(BF16)
    dmessage = (mul(gout[...], wm[...], 1, 1) / degree).astype(BF16)
    for p in range(nd):
        sback[p] = mul(counts[:, p * cap : (p + 1) * cap], dmessage, 0, 0).astype(BF16)
    for k in range(1, nd):
        swap(sback, rback, bsend, brecv, k, False).start()
    rback[my_dom] = sback[my_dom]

    if nb > 2:
        line_recv(0)
        line_send(1, True)
    for k in range(1, nd):
        swap(sbuf, rbuf, asend, arecv, k, True).wait_recv()
    table = rbuf[...].reshape(nd * cap, -1)
    mean_out[...] = (mul(counts, table, 1, 0) / degree).astype(BF16)
    for step in range(2, nb - 1):
        line_recv(step - 1)
        line_send(step, True)
    for k in range(1, nd):
        swap(sback, rback, bsend, brecv, k, True).wait_recv()
    back = rback[...].reshape(nd * cap, -1)
    halo_out[...] = mul(onehot[...], back, 1, 0)
    line_recv(nb - 2)
    for step in range(nb - 1):
        line_send(step, False)
    for k in range(1, nd):
        swap(sbuf, rbuf, asend, arecv, k, False).wait_send()
        swap(sback, rback, bsend, brecv, k, False).wait_send()
    for c in local:
        c.wait()


def exchange(nd, nb, feat, gout, gain, wm, meta, sidx, esrc, edst):
    rows, width = feat.shape
    cap = sidx.shape[1]
    vmem = pl.BlockSpec(memory_space=pltpu.VMEM)
    anywhere = pl.BlockSpec(memory_space=pl.ANY)
    slots = pltpu.VMEM((nd, cap, width), BF16)
    dma = pltpu.SemaphoreType.DMA
    return pl.pallas_call(
        partial(exchange_kernel, nd, nb),
        out_shape=[
            jax.ShapeDtypeStruct((nb, rows, width), BF16),
            jax.ShapeDtypeStruct((nb, rows, width), BF16),
            jax.ShapeDtypeStruct((nb, 8, rows), jnp.int32),
            jax.ShapeDtypeStruct((rows, width), BF16),
            jax.ShapeDtypeStruct((rows, width), F32),
        ],
        in_specs=[vmem] * 8,
        out_specs=[anywhere] * 3 + [vmem] * 2,
        scratch_shapes=[
            slots, slots, slots, slots,
            pltpu.VMEM((rows, nd * cap), F32),
            pltpu.VMEM((rows, nd * cap), BF16),
            dma((3,)),
            dma((2, nb, 3)), dma((2, nb, 3)),
            dma((nd,)), dma((nd,)), dma((nd,)), dma((nd,)),
        ],
        compiler_params=params(0),
    )(feat, gout, gain, wm, meta, sidx, esrc, edst)


def attend_kernel(
    feats, feat, gout, gain, wq, wk, wv, wo, mean, wm, key_labels, own_labels,
    layer, normed_all, attn_t, dq_t, stats,
    k_t, v_t, q_t, ga_t, bias, dq_f,
):
    x = feats[...].astype(F32)
    normed_all[...] = (x * row_scale(x) * gain[...]).astype(BF16)
    x = feat[...].astype(F32)
    normed = (x * row_scale(x) * gain[...]).astype(BF16)
    keys, _ = head_norm(mul(wk[...], normed_all[...], 0, 1))
    k_t[...] = keys.reshape(k_t.shape).astype(BF16)
    v_t[...] = mul(wv[...], normed_all[...], 0, 1).astype(BF16)
    queries, q_scaling = head_norm(mul(wq[...], normed, 0, 1))
    q_t[...] = (queries * SCALE).reshape(q_t.shape).astype(BF16)
    ga_t[...] = mul(wo[...], gout[...], 1, 1)
    bias[...] = jnp.where(key_labels[...] == own_labels[...], -SHIFT, MASKED)
    for h in range(HEADS):
        part = slice(h * HEAD_DIM, (h + 1) * HEAD_DIM)
        kh, vh, qh, ga = k_t[part, :], v_t[part, :], q_t[part, :], ga_t[part, :]
        weights = jnp.exp(mul(kh, qh, 0, 0) + bias[...])
        inv = 1.0 / jnp.sum(weights, axis=0, keepdims=True)
        attn = (mul(vh, weights.astype(BF16), 1, 0) * inv).astype(BF16)
        attn_t[part, :] = attn
        correction = jnp.sum(ga * attn.astype(F32), axis=0, keepdims=True) * inv
        stats[h : h + 1, :] = inv
        stats[HEADS + h : HEADS + h + 1, :] = correction
        dots = mul(vh, (ga * inv).astype(BF16), 0, 0)
        slopes = (weights * (dots - correction)).astype(BF16)
        dq_f[part, :] = mul(kh, slopes, 1, 0) * SCALE
    dq_t[...] = head_norm_pull(queries, q_scaling, dq_f[...]).astype(BF16)
    out = x + mul(mean[...], wm[...], 1, 0) + mul(attn_t[...], wo[...], 0, 0)
    layer[...] = out.astype(BF16)


def attend(feats, feat, gout, gain, wq, wk, wv, wo, mean, wm, key_labels, own_labels):
    rows, width = feat.shape
    total = feats.shape[0]
    vmem = pl.BlockSpec(memory_space=pltpu.VMEM)
    return pl.pallas_call(
        attend_kernel,
        out_shape=[
            jax.ShapeDtypeStruct((rows, width), BF16),
            jax.ShapeDtypeStruct((total, width), BF16),
            jax.ShapeDtypeStruct((width, rows), BF16),
            jax.ShapeDtypeStruct((width, rows), BF16),
            jax.ShapeDtypeStruct((2 * HEADS, rows), F32),
        ],
        in_specs=[vmem] * 12,
        out_specs=[vmem] * 5,
        scratch_shapes=[
            pltpu.VMEM((width, total), BF16),
            pltpu.VMEM((width, total), BF16),
            pltpu.VMEM((width, rows), BF16),
            pltpu.VMEM((width, rows), F32),
            pltpu.VMEM((total, rows), F32),
            pltpu.VMEM((width, rows), F32),
        ],
        compiler_params=params(),
    )(feats, feat, gout, gain, wq, wk, wv, wo, mean, wm, key_labels, own_labels)


def share_kernel(nb, x, out, own_sem, send, recv):
    me = lax.axis_index("blk")
    barrier = pltpu.get_barrier_semaphore()
    for k in range(1, nb):
        pl.semaphore_signal(
            barrier, inc=1, device_id={"blk": lax.rem(me + k, nb)}, device_id_type=MESH
        )
    pl.semaphore_wait(barrier, nb - 1)
    for k in range(1, nb):
        to = lax.rem(me + k, nb)
        remote(x, out.at[me], send.at[k], recv.at[k], "blk", to).start()
    out[me] = x[...]
    for k in range(1, nb):
        to = lax.rem(me + k, nb)
        origin = lax.rem(me + nb - k, nb)
        remote(x, out.at[origin], send.at[k], recv.at[k], "blk", to).wait()


def share(nb, x):
    vmem = pl.BlockSpec(memory_space=pltpu.VMEM)
    dma = pltpu.SemaphoreType.DMA
    return pl.pallas_call(
        partial(share_kernel, nb),
        out_shape=jax.ShapeDtypeStruct((nb,) + x.shape, x.dtype),
        in_specs=[vmem],
        out_specs=vmem,
        scratch_shapes=[dma((1,)), dma((nb,)), dma((nb,))],
        compiler_params=params(1),
    )(x)


def gradient_kernel(
    nb,
    normed_all, gouts, stats, feat, gout, gain, wq, wk, wv, wo,
    own_labels, query_labels, attn_t, dq_t, mean, halo,
    fgrad, wgrads, gain_out,
    q_t, gh_t, v_t, k_t, bias, dk_f, dv_f,
):
    width = wq.shape[0]
    half = width // 2
    x = feat[...].astype(F32)
    scaling = row_scale(x)
    xs = x * scaling
    normed = (xs * gain[...]).astype(BF16)
    queries, _ = head_norm(mul(wq[...], normed_all[...], 0, 1))
    q_t[...] = (queries * SCALE).reshape(q_t.shape).astype(BF16)
    inv = jnp.concatenate([stats[b, :HEADS, :] for b in range(nb)], axis=1)
    correction = jnp.concatenate([stats[b, HEADS:, :] for b in range(nb)], axis=1)
    ga = mul(wo[...], gouts[...], 1, 1).reshape(HEADS, HEAD_DIM, -1)
    gh_t[...] = (ga * inv[:, None, :]).reshape(gh_t.shape).astype(BF16)
    keys, k_scaling = head_norm(mul(wk[...], normed, 0, 1))
    k_t[...] = keys.reshape(k_t.shape).astype(BF16)
    v_t[...] = mul(wv[...], normed, 0, 1).astype(BF16)
    bias[...] = jnp.where(own_labels[...] == query_labels[...], -SHIFT, MASKED)
    for h in range(HEADS):
        part = slice(h * HEAD_DIM, (h + 1) * HEAD_DIM)
        kh, vh, qh, gh = k_t[part, :], v_t[part, :], q_t[part, :], gh_t[part, :]
        weights = jnp.exp(mul(kh, qh, 0, 0) + bias[...])
        dots = mul(vh, gh, 0, 0)
        slopes = (weights * (dots - correction[h : h + 1, :])).astype(BF16)
        dk_f[part, :] = mul(qh, slopes, 1, 1)
        dv_f[part, :] = mul(gh, weights.astype(BF16), 1, 1)
    dk_t = head_norm_pull(keys, k_scaling, dk_f[...]).astype(BF16)
    dv_t = dv_f[...].astype(BF16)
    dq = dq_t[...]
    dnormed = (mul(wq[...], dq, 1, 0) + mul(wk[...], dk_t, 1, 0) + mul(wv[...], dv_t, 1, 0)).T
    dnormed = dnormed + halo[...]
    dscaled = dnormed * gain[...]
    gain_out[...] = jnp.broadcast_to(
        jnp.sum(dnormed * xs, axis=0, keepdims=True), gain_out.shape
    )
    dx = scaling * (dscaled - xs * jnp.mean(dscaled * xs, axis=-1, keepdims=True))
    g = gout[...]
    fgrad[...] = (g.astype(F32) + dx).astype(BF16)

    def put(n, value):
        value = value.astype(BF16)
        wgrads[0, n * width : (n + 1) * width, :] = value[:, :half]
        wgrads[1, n * width : (n + 1) * width, :] = value[:, half:]

    for n, d in enumerate((dq, dk_t, dv_t)):
        put(n, mul(normed, d, 0, 1))
    put(3, mul(attn_t[...], g, 1, 0))
    put(4, mul(mean[...], g, 0, 0))


def gradients(nb, *args):
    normed_all, feat = args[0], args[3]
    total, width = normed_all.shape
    rows = feat.shape[0]
    vmem = pl.BlockSpec(memory_space=pltpu.VMEM)
    return pl.pallas_call(
        partial(gradient_kernel, nb),
        out_shape=[
            jax.ShapeDtypeStruct((rows, width), BF16),
            jax.ShapeDtypeStruct((2, 5 * width, width // 2), BF16),
            jax.ShapeDtypeStruct((8, width), F32),
        ],
        in_specs=[vmem] * len(args),
        out_specs=[vmem] * 3,
        scratch_shapes=[
            pltpu.VMEM((width, total), BF16),
            pltpu.VMEM((width, total), BF16),
            pltpu.VMEM((width, rows), BF16),
            pltpu.VMEM((width, rows), BF16),
            pltpu.VMEM((rows, total), F32),
            pltpu.VMEM((width, rows), F32),
            pltpu.VMEM((width, rows), F32),
        ],
        compiler_params=params(),
    )(*args)


def plan(nd, nb, rows):
    dom_bits = [1 << i for i in range(nd.bit_length() - 1)]
    blk_bits = [1 << i for i in range(nb.bit_length() - 1)]
    orders = (dom_bits, dom_bits[:1] + dom_bits[:0:-1])
    plans = []
    for order in orders:
        held, steps = rows, []
        for axis, bit in [("dom", b) for b in order] + [("blk", b) for b in blk_bits[::-1]]:
            halves = held % 32 == 0
            steps.append((axis, bit, held, halves))
            held = held // 2 if halves else held
        plans.append(steps)
    return plans


def reduce_kernel(plans, w, g, out, gsum, acc, gacc, *rest):
    n = len(plans[0])
    recvs, (grecv, send, recv, asend, arecv, gsend, grsem) = rest[: 2 * n], rest[2 * n :]
    index = {"dom": lax.axis_index("dom"), "blk": lax.axis_index("blk")}

    def bit_of(axis, bit):
        return lax.rem(index[axis] // bit, 2)

    def peer_of(axis, bit):
        return index[axis] + bit - 2 * bit * bit_of(axis, bit)

    barrier = pltpu.get_barrier_semaphore()
    for axis, bit, _, _ in plans[0]:
        pl.semaphore_signal(
            barrier, inc=1, device_id={axis: peer_of(axis, bit)}, device_id_type=MESH
        )
    pl.semaphore_wait(barrier, n)

    def rows_at(first, count):
        return pl.ds(pl.multiple_of(first, 16), count)

    gacc[0] = g[...]
    first = [0, 0]
    history = [[], []]
    for s in range(n):
        copies = []
        for half in range(2):
            axis, bit, held, halves = plans[half][s]
            mine = bit_of(axis, bit)
            peer = peer_of(axis, bit)
            count = held // 2 if halves else held
            away = first[half] + (1 - mine) * count if halves else first[half]
            keep = first[half] + mine * count if halves else first[half]
            src = (w if s == 0 else acc.at[s - 1]).at[half, rows_at(away, count), :]
            c = remote(src, recvs[2 * s + half], send.at[s, half], recv.at[s, half], axis, peer)
            c.start()
            copies.append((c, keep, count))
            history[half].append((axis, peer, keep, count, halves))
            first[half] = keep
        axis, bit, _, _ = plans[0][s]
        gc = remote(
            gacc.at[s], grecv.at[s], gsend.at[s], grsem.at[s], axis, peer_of(axis, bit)
        )
        gc.start()
        for half, (c, keep, count) in enumerate(copies):
            c.wait_recv()
            src = w if s == 0 else acc.at[s - 1]
            total = (
                src[half, rows_at(keep, count), :].astype(F32)
                + recvs[2 * s + half][...].astype(F32)
            ).astype(BF16)
            if s == n - 1:
                out[half, rows_at(keep, count), :] = total
            else:
                acc[s, half, rows_at(keep, count), :] = total
        gc.wait()
        gacc[s + 1] = gacc[s] + grecv[s]
        for c, _, _ in copies:
            c.wait_send()
    gsum[...] = gacc[n]
    for s in range(n - 1, -1, -1):
        copies = []
        for half in range(2):
            axis, peer, keep, count, halves = history[half][s]
            if not halves:
                continue
            place = out.at[half, rows_at(keep, count), :]
            c = remote(place, place, asend.at[s, half], arecv.at[s, half], axis, peer)
            c.start()
            copies.append(c)
        for c in copies:
            c.wait()


def reduce_all(nd, nb, w, g):
    plans = plan(nd, nb, w.shape[1])
    n = len(plans[0])
    vmem = pl.BlockSpec(memory_space=pltpu.VMEM)
    dma = pltpu.SemaphoreType.DMA
    bufs = []
    for s in range(n):
        for half in range(2):
            _, _, held, halves = plans[half][s]
            bufs.append(pltpu.VMEM((held // 2 if halves else held, w.shape[2]), BF16))
    return pl.pallas_call(
        partial(reduce_kernel, plans),
        out_shape=[
            jax.ShapeDtypeStruct(w.shape, BF16),
            jax.ShapeDtypeStruct(g.shape, F32),
        ],
        in_specs=[vmem] * 2,
        out_specs=[vmem] * 2,
        scratch_shapes=[
            pltpu.VMEM((n - 1,) + w.shape, BF16),
            pltpu.VMEM((n + 1,) + g.shape, F32),
        ]
        + bufs
        + [pltpu.VMEM((n,) + g.shape, F32)]
        + [dma((n, 2))] * 4
        + [dma((n,))] * 2,
        compiler_params=params(2),
    )(w, g)


def local(
    node_features, norm_gain, w_query, w_key, w_value, w_out, w_message, node_cluster,
    block_pattern, send_rows, send_counts, edge_src, edge_dst, out_grad,
):
    rows, width = node_features.shape
    nd = lax.axis_size("dom")
    nb = lax.axis_size("blk")
    me = lax.axis_index("blk")
    cap = send_rows.shape[1]
    gain = norm_gain.reshape(1, width)
    live = jnp.arange(cap, dtype=jnp.int32)[None, :] < send_counts[:, None]
    sidx = jnp.where(live, send_rows, -1)
    pattern_row = jnp.pad(block_pattern, ((0, 0), (0, rows - nb)))
    meta = jnp.concatenate(
        [node_cluster[None, :], pattern_row, jnp.zeros((6, rows), jnp.int32)], axis=0
    )
    feats, gouts, metas, mean, halo = exchange(
        nd, nb, node_features, out_grad, gain, w_message, meta, sidx,
        edge_src.reshape(-1, EDGE_PART), edge_dst.reshape(-1, EDGE_PART),
    )
    labels = metas[:, 0, :]
    key_labels = jnp.where(block_pattern[0][:, None] == 1, labels, -1).reshape(-1, 1)
    towards_me = lax.dynamic_slice_in_dim(metas[:, 1, :], me, 1, 1)
    query_labels = jnp.where(towards_me == 1, labels, -1).reshape(1, -1)
    feats = feats.reshape(nb * rows, width)
    gouts = gouts.reshape(nb * rows, width)
    layer_out, normed_all, attn_t, dq_t, stats = attend(
        feats, node_features, out_grad, gain, w_query, w_key, w_value, w_out, mean, w_message,
        key_labels, node_cluster.reshape(1, rows),
    )
    stats = share(nb, stats)
    feature_grad, wgrads, gain_part = gradients(
        nb, normed_all, gouts, stats, node_features, out_grad, gain, w_query, w_key, w_value,
        w_out, node_cluster.reshape(rows, 1), query_labels, attn_t, dq_t, mean, halo,
    )
    sums, gain_sum = reduce_all(nd, nb, wgrads, gain_part)
    sums = sums.astype(F32).reshape(2, 5, width, width // 2)
    weight_sums = jnp.concatenate([sums[0], sums[1]], axis=-1)
    return (layer_out, feature_grad, weight_sums, gain_sum[0])


def solution(mesh):
    nodes = P(("dom", "blk"))
    wide = P(("dom", "blk"), None)
    placed = (
        wide, P(), P(), P(), P(), P(), P(), nodes, wide, wide, nodes, nodes, nodes, wide,
    )
    return jax.shard_map(
        local,
        mesh=mesh,
        in_specs=placed,
        out_specs=(wide, wide, P(), P()),
        check_vma=False,
    )
```

time: 396 us -> 157 us (0.40)
  waiting for transfers between devices: 145 us -> 0 us
  Pallas kernels: 0 us -> 139 us
  other arithmetic: 70.1 us -> 8.1 us
  blocking collectives: 51.6 us -> 0 us
  local copies, waits for them, and re-layouts: 57.7 us -> 9.14 us
  matrix products: 44.4 us -> 0 us
  between operations: 14.7 us -> 0.69 us
  starting transfers between devices: 8.7 us -> 0 us
    pallas_call x0 -> x5, Pallas kernels: none -> 139 us  [the longest x1 59.7 us: reduce_all(): pl.pallas_call(partial(reduce_kernel, plans), out_shape=[jax.ShapeDtypeSt...]
    psum x1 -> x0, waiting for transfers between devices: 92.6 us -> none  [local(): weight_sums, gain_sum = lax.psum((weight_terms, gain_term), ('dom', 'blk'))]
    scatter-add x3 -> x0, other arithmetic: 57.9 us -> none  [the longest x1 28.8 us: local(): jax.ops.segment_sum(jnp.ones(edge_dst.shape, jnp.float32), edge_dst, row_...]
    dot_general x44 -> x0, matrix products: 44.4 us -> none  [the longest x8 9.38 us: block_weights(): jnp.einsum('rhe,khe->hrk', query_heads, key_heads, preferred_element_type...]
    psum x1 -> x0, blocking collectives: 38.9 us -> none  [local(): weight_sums, gain_sum = lax.psum((weight_terms, gain_term), ('dom', 'blk'))]
    all_gather x2 -> x0, waiting for transfers between devices: 36.9 us -> none  [the longest x1 24.3 us: local(): lax.all_gather(value_flat, 'blk', axis=0, tiled=True)]
    reduce_scatter x2 -> x0, waiting for transfers between devices: 15.1 us -> none  [the longest x1 15.1 us: local(): lax.psum_scatter(value_terms.reshape(block_count * row_count, feat_width)...]
    unnamed x94 -> x5, local copies, waits for them, and re-layouts: 14.9 us -> 0.45 us
  transfers between devices with their start and end apart: 7 -> 0, of which waited for: 4 -> 0; matrix products, arithmetic and copies ran while one was open for 24% -> 0% of each run, Pallas kernels for 0% -> 0%
where the time goes in v1:
time: 157 us; the launch traced here: 156 us
  Pallas kernels  139 us (89%)
  local copies, waits for them, and re-layouts  9.14 us (6%)
  other arithmetic  8.1 us (5%)
    pallas_call x1, Pallas kernels, reduce_all(): pl.pallas_call(partial(reduce_kernel, plans), out_shape=[jax.ShapeDtypeSt...  59.7 us
    pallas_call x1, Pallas kernels, exchange(): pl.pallas_call(partial(exchange_kernel, nd, nb), out_shape=[jax.ShapeDtyp...  47.8 us
    pallas_call x1, Pallas kernels, gradients(): pl.pallas_call(partial(gradient_kernel, nb), out_shape=[jax.ShapeDtypeStr...  12.1 us
    pallas_call x1, Pallas kernels, attend(): pl.pallas_call(attend_kernel, out_shape=[jax.ShapeDtypeStruct((rows, widt...  11.9 us
    pallas_call x1, Pallas kernels, share(): pl.pallas_call(partial(share_kernel, nb), out_shape=jax.ShapeDtypeStruct(...  6.95 us

profile of v1, /device:TPU:0, one launch (start us, length us, event | category | flops | bytes accessed | tf_op | source)
XLA Modules:
  0.0 156.4 jit_solution(5819069908256583590)
XLA Ops:
  0.6 0.7 compare_bitcast_fusion
  1.3 0.1 broadcast_bitcast_fusion.1
  1.4 0.1 pad.9.clone
  1.5 1.4 fusion.1.sidx
  2.8 1.4 fusion.meta
  4.2 1.3 reshape.93.esrc
  5.5 1.3 reshape.94.edst
  6.8 0.3 copy.22
  7.1 1.5 copy.20.own_labels
  8.6 47.8 %shard_map.165 = (bf16[4,256,512]{2,1,0:T(8,128)(2,1)}, bf16[4,256,512]{2,1,0:T(8,128)(2,1)}, s32[4,8,256]{2,1,0:T(8,128)}, bf16[256,512]{1,0:T(8,128)(2,1)}, f32[256,512]{1,0:T(8,128)}) custom-call(bf16[256,512]{1,0:T(8,128)(2,1)} %feat.5, bf16[256,512]{1,0:T(8,128)(2,1)} %gout.5, f32[1,512]{1,0:T(1,128)} %bitcast.28, bf16[512,512]{1,0:T(8,128)(2,1)} %wm.3, ...), custom_call_target="tpu_custom_call" | custom-call | tf_op jit(solution)/shard_map/pallas_call | solution.py:190
  56.4 0.8 fusion.3
  57.3 0.2 compare_reduce_fusion
  57.5 0.1 broadcast_bitcast_fusion
  57.6 0.6 broadcast_select_fusion.query_labels
  58.2 0.2 copy.19
  58.4 0.9 bitcast_select_fusion.key_labels
  59.3 11.9 %shard_map.166 = (bf16[256,512]{1,0:T(8,128)(2,1)}, bf16[1024,512]{1,0:T(8,128)(2,1)}, bf16[512,256]{1,0:T(8,128)(2,1)}, bf16[512,256]{1,0:T(8,128)(2,1)}, f32[16,256]{1,0:T(8,128)}) custom-call(bf16[1024,512]{1,0:T(8,128)(2,1)} %bitcast.25, bf16[256,512]{1,0:T(8,128)(2,1)} %feat.5, bf16[256,512]{1,0:T(8,128)(2,1)} %gout.5, f32[1,512]{1,0:T(1,128)} %bitcast.29, ...), custom_call_target="tpu_custom_call" | custom-call | tf_op jit(solution)/shard_map/pallas_call | solution.py:251
  71.2 7.0 %shard_map.167.stats = f32[4,16,256]{2,1,0:T(8,128)} custom-call(f32[16,256]{1,0:T(8,128)} %get-tuple-element.25.x), custom_call_target="tpu_custom_call" | custom-call | tf_op jit(solution)/shard_map/pallas_call | solution.py:295
  78.2 12.1 %shard_map.168 = (bf16[256,512]{1,0:T(8,128)(2,1)}, bf16[2,2560,256]{2,1,0:T(8,128)(2,1)}, f32[8,512]{1,0:T(8,128)}) custom-call(bf16[1024,512]{1,0:T(8,128)(2,1)} %get-tuple-element.23.normed_all, bf16[1024,512]{1,0:T(8,128)(2,1)} %bitcast.24, f32[4,16,256]{2,1,0:T(8,128)} %shard_map.167.stats, bf16[256,512]{1,0:T(8,128)(2,1)} %feat.5, ...), custom_call_target="tpu_custom_call" | custom-call | tf_op jit(solution)/shard_map/pallas_call | solution.py:365
  90.3 59.7 %shard_map.169 = (bf16[2,2560,256]{2,1,0:T(8,128)(2,1)}, f32[8,512]{1,0:T(8,128)}) custom-call(bf16[2,2560,256]{2,1,0:T(8,128)(2,1)} %get-tuple-element.30.w, f32[8,512]{1,0:T(8,128)} %get-tuple-element.31.g), custom_call_target="tpu_custom_call" | custom-call | tf_op jit(solution)/shard_map/pallas_call | solution.py:486
  150.0 1.3 slice.21
  151.3 2.1 %fusion.2 = (f32[1,2560,256]{2,1,0:T(8,128)S(1)}, f32[1,2560,256]{2,1,0:T(8,128)S(1)}) fusion(bf16[2,2560,256]{2,1,0:T(8,128)(2,1)} %get-tuple-element.32), kind=kLoop, calls=%fused_computation.11 | loop fusion | bytes 10485760 | tf_op jit(solution)/shard_map/slice | solution.py:543
  153.4 3.0 %pad_maximum_fusion = f32[5,512,512]{2,1,0:T(8,128)} fusion(f32[5,512,256]{2,1,0:T(8,128)S(1)} %bitcast.23, f32[5,512,256]{2,1,0:T(8,128)S(1)} %bitcast.22), kind=kLoop, calls=%fused_computation | loop fusion | flops 1310720 | bytes 10485760 | tf_op jit(solution)/shard_map/concatenate | solution.py:543
  (3 shorter events, 0.0 us)

commit v2 on v1

v2 whole, which is shorter than its diff:
```python
from functools import partial

import jax
import jax.numpy as jnp
from jax import lax
from jax.experimental import pallas as pl
from jax.experimental.pallas import tpu as pltpu
from jax.sharding import PartitionSpec as P

HEADS = 8
HEAD_DIM = 64
SCALE = 8.0 / HEAD_DIM
SHIFT = 8.0
EPS = 1e-06
MASKED = -1e30
EDGE_PART = 512
MESH = pl.DeviceIdType.MESH
F32 = jnp.float32
BF16 = jnp.bfloat16


def params(collective_id=None):
    return pltpu.CompilerParams(
        vmem_limit_bytes=56 * 1024 * 1024,
        collective_id=collective_id,
        has_side_effects=collective_id is not None,
    )


def mul(a, b, ca, cb):
    return lax.dot_general(a, b, (((ca,), (cb,)), ((), ())), preferred_element_type=F32)


def row_scale(x):
    return lax.rsqrt(jnp.mean(x * x, axis=-1, keepdims=True) + EPS)


def head_norm(x):
    view = x.reshape(HEADS, HEAD_DIM, x.shape[1])
    scaling = lax.rsqrt(jnp.mean(view * view, axis=1, keepdims=True) + EPS)
    return view * scaling, scaling


def head_norm_pull(y, scaling, dy):
    dy = dy.reshape(y.shape)
    dx = scaling * (dy - y * jnp.mean(y * dy, axis=1, keepdims=True))
    return dx.reshape(-1, y.shape[2])


def remote(src, dst, send, recv, axis, peer):
    return pltpu.make_async_remote_copy(
        src_ref=src, dst_ref=dst, send_sem=send, recv_sem=recv,
        device_id={axis: peer}, device_id_type=MESH,
    )


def plan(nd, nb, rows, flip):
    dom_bits = [1 << i for i in range(nd.bit_length() - 1)]
    blk_bits = [1 << i for i in range(nb.bit_length() - 1)]
    if flip:
        dom_bits = dom_bits[:1] + dom_bits[:0:-1]
    steps = []
    for axis, bit in [("dom", b) for b in dom_bits] + [("blk", b) for b in blk_bits]:
        halves = rows % 32 == 0
        rows = rows // 2 if halves else rows
        steps.append((axis, bit, rows, halves))
    return steps


FLIPS = (True, False, True, False, True)
PIECES = len(FLIPS)


def layer_kernel(
    nd, nb,
    feat, gout, gain, wq, wk, wv, wo, wm, labels, sidx, esrc, edst, live_counts, pattern,
    layer, fgrad, sums, gsum,
    feats, gouts, metas, mine, sbuf, rbuf, sback, rback, cnt, onehot,
    k_t, v_t, q_t, q_own, ga_t, attn_t, mean_rows, bias, bias_own, dq_f, dk_f, dv_f, gh_t,
    stats, all_stats, terms, gacc, grecv,
    zsend, zrecv, asend, arecv, bsend, brecv, ssend, srecv,
    rsend, rrecv, gsend, grsem, hsend, hrecv,
    *buffers,
):
    me = lax.axis_index("blk")
    my_dom = lax.axis_index("dom")
    index = {"dom": my_dom, "blk": me}
    rows, width = feat.shape
    cap = sidx.shape[1]
    plans = [plan(nd, nb, width, f) for f in FLIPS]
    n = len(plans[0])
    acc = [[buffers[2 * (p * n + s)] for s in range(n)] for p in range(PIECES)]
    got = [[buffers[2 * (p * n + s) + 1] for s in range(n)] for p in range(PIECES)]

    barrier = pltpu.get_barrier_semaphore()
    for axis, size in (("dom", nd), ("blk", nb)):
        for k in range(1, size):
            pl.semaphore_signal(
                barrier, inc=1, device_id={axis: lax.rem(index[axis] + k, size)},
                device_id_type=MESH,
            )

    own_labels = labels[...]
    mine[...] = jnp.zeros_like(mine)
    mine[0:1, :] = own_labels
    for b in range(nb):
        mine[1 + b : 2 + b, :] = jnp.where(pattern[0, b] == 1, own_labels, -1)
    pl.semaphore_wait(barrier, nd - 1 + nb - 1)

    streams = ((feat, feats), (gout, gouts), (mine, metas))

    def line_copy(step, way, k, block):
        src, dst = streams[k]
        if step > 0:
            src = dst.at[block]
        peer = me + 1 if way == 0 else me - 1
        return remote(
            src, dst.at[block], zsend.at[way, step, k], zrecv.at[way, step, k], "blk", peer
        )

    def line_send(step, kinds, start=True):
        for way in range(2):
            sends = (me + 1 < nb) & (me - step >= 0) if way == 0 else (me >= 1) & (me + step < nb)
            block = me - step if way == 0 else me + step

            @pl.when(sends)
            def _():
                for k in kinds:
                    c = line_copy(step, way, k, block)
                    if start:
                        c.start()
                    else:
                        c.wait_send()

    def line_recv(step, kinds):
        for way in range(2):
            block = me - 1 - step if way == 0 else me + 1 + step
            comes = block >= 0 if way == 0 else block < nb

            @pl.when(comes)
            def _():
                for k in kinds:
                    line_copy(step, way, k, block).wait_recv()

    def swap(src, dst, send, recv, k, incoming):
        to = lax.rem(my_dom + k, nd)
        origin = lax.rem(my_dom + nd - k, nd)
        return remote(
            src.at[to], dst.at[origin if incoming else my_dom], send.at[k], recv.at[k], "dom", to
        )

    stage = [-1] * PIECES
    first = [None] * PIECES
    history = [[] for _ in range(PIECES)]

    def aligned(start, count):
        return pl.ds(pl.multiple_of(start, 16), count)

    def peer_of(axis, bit):
        mine_bit = lax.rem(index[axis] // bit, 2)
        return mine_bit, index[axis] + bit - 2 * bit * mine_bit

    def gain_copy(s):
        axis, bit, _, _ = plans[1][s]
        return remote(gacc.at[s], grecv.at[s], gsend.at[s], grsem.at[s], axis, peer_of(axis, bit)[1])

    def reduce_copy(p, s):
        axis, bit, count, halves = plans[p][s]
        bit_set, peer = peer_of(axis, bit)
        src = terms.at[p] if s == 0 else acc[p][s - 1]
        away = (1 - bit_set) * count if halves else 0
        keep = bit_set * count if halves else 0
        c = remote(
            src.at[aligned(away, count), :], got[p][s], rsend.at[p, s], rrecv.at[p, s], axis, peer
        )
        return c, src, keep

    def spread_copy(p, s):
        axis, peer, start, count = history[p][s]
        place = sums.at[aligned(p * width + start, count), :]
        return remote(place, place, hsend.at[p, s], hrecv.at[p, s], axis, peer)

    def begin(p):
        stage[p] = 0
        first[p] = 0
        reduce_copy(p, 0)[0].start()

    def advance(p):
        s = stage[p]
        if s < n:
            c, src, keep = reduce_copy(p, s)
            axis, bit, count, halves = plans[p][s]
            c.wait_recv()
            total = (
                src[aligned(keep, count), :].astype(F32) + got[p][s][...].astype(F32)
            ).astype(BF16)
            first[p] = first[p] + keep
            history[p].append((axis, peer_of(axis, bit)[1], first[p], count))
            if s == n - 1:
                sums[aligned(p * width + first[p], count), :] = total
            else:
                acc[p][s][...] = total
                reduce_copy(p, s + 1)[0].start()
        else:
            spread_copy(p, 2 * n - 1 - s).wait_recv()
        s += 1
        while n <= s < 2 * n and not plans[p][2 * n - 1 - s][3]:
            s += 1
        stage[p] = s
        if n <= s < 2 * n:
            spread_copy(p, 2 * n - 1 - s).start()

    def advance_if(p):
        if 0 <= stage[p] < 2 * n:
            advance(p)

    def settle(p):
        for s in range(n):
            reduce_copy(p, s)[0].wait_send()
            if plans[p][s][3]:
                spread_copy(p, s).wait_send()

    line_send(0, (0, 2))
    feats[me] = feat[...]
    gouts[me] = gout[...]
    metas[me] = mine[...]

    x = feat[...].astype(F32)
    scaling = row_scale(x)
    normed = (x * scaling * gain[...]).astype(BF16)
    row_ids = lax.broadcasted_iota(jnp.int32, (rows, cap), 0)
    lane_ids = lax.broadcasted_iota(jnp.int32, (1, cap), 1)
    for p in range(nd):
        picks = jnp.where(lane_ids < live_counts[p], sidx[p : p + 1, :], -1)
        hot = jnp.where(row_ids == picks, 1.0, 0.0).astype(BF16)
        onehot[:, p * cap : (p + 1) * cap] = hot
        sbuf[p] = mul(hot, normed, 0, 0).astype(BF16)
    for k in range(1, nd):
        swap(sbuf, rbuf, asend, arecv, k, False).start()
    rbuf[my_dom] = sbuf[my_dom]

    slot_ids = lax.broadcasted_iota(jnp.int32, (nd * cap, EDGE_PART), 0)
    dst_ids = lax.broadcasted_iota(jnp.int32, (rows, EDGE_PART), 0)
    cnt[...] = jnp.zeros_like(cnt)

    def count_edges(c, carry):
        at = pl.ds(pl.multiple_of(c * EDGE_PART, EDGE_PART), EDGE_PART)
        hot_src = jnp.where(slot_ids == esrc[:, at], 1.0, 0.0).astype(BF16)
        hot_dst = jnp.where(dst_ids == edst[:, at], 1.0, 0.0).astype(BF16)
        cnt[...] += mul(hot_dst, hot_src, 1, 1)
        return carry

    lax.fori_loop(0, esrc.shape[1] // EDGE_PART, count_edges, 0)
    counts = cnt[...]
    degree = jnp.maximum(jnp.sum(counts, axis=1, keepdims=True), 1.0)
    counts = counts.astype(BF16)
    if nb > 2:
        line_recv(0, (0, 2))
        line_send(1, (0, 2))
    dmessage = (mul(gout[...], wm[...], 1, 1) / degree).astype(BF16)
    for p in range(nd):
        sback[p] = mul(counts[:, p * cap : (p + 1) * cap], dmessage, 0, 0).astype(BF16)
    for k in range(1, nd):
        swap(sback, rback, bsend, brecv, k, False).start()
    rback[my_dom] = sback[my_dom]

    queries, q_scaling = head_norm(mul(wq[...], normed, 0, 1))
    q_own[...] = (queries * SCALE).reshape(q_own.shape).astype(BF16)
    ga_t[...] = mul(wo[...], gout[...], 1, 1)
    for k in range(1, nd):
        swap(sbuf, rbuf, asend, arecv, k, True).wait_recv()
    mean = (mul(counts, rbuf[...].reshape(nd * cap, width), 1, 0) / degree).astype(BF16)
    mean_rows[...] = mean
    terms[4] = mul(mean, gout[...], 0, 0).astype(BF16)
    begin(4)
    for step in range(2, nb - 1):
        line_recv(step - 1, (0, 2))
        line_send(step, (0, 2))
    line_recv(nb - 2, (0, 2))
    line_send(0, (1,))

    x_all = feats[...].reshape(nb * rows, width).astype(F32)
    normed_all = (x_all * row_scale(x_all) * gain[...]).astype(BF16)
    keys, _ = head_norm(mul(wk[...], normed_all, 0, 1))
    k_t[...] = keys.reshape(k_t.shape).astype(BF16)
    v_t[...] = mul(wv[...], normed_all, 0, 1).astype(BF16)
    all_queries, _ = head_norm(mul(wq[...], normed_all, 0, 1))
    q_t[...] = (all_queries * SCALE).reshape(q_t.shape).astype(BF16)
    own_row = own_labels.astype(F32)
    own_column = jnp.broadcast_to(own_row, (rows, rows)).T
    for b in range(nb):
        at = slice(b * rows, (b + 1) * rows)
        row = jnp.where(pattern[0, b] == 1, metas[b, 0:1, :], -1).astype(F32)
        column = jnp.broadcast_to(row, (rows, rows)).T
        bias[at, :] = jnp.where(column == own_row, -SHIFT, MASKED)
        towards = metas[b, pl.ds(1 + me, 1), :].astype(F32)
        bias_own[:, at] = jnp.where(own_column == towards, -SHIFT, MASKED)
    pending = list(range(1, nb - 1))
    for h in range(HEADS):
        part = slice(h * HEAD_DIM, (h + 1) * HEAD_DIM)
        kh, vh, qh, ga = k_t[part, :], v_t[part, :], q_own[part, :], ga_t[part, :]
        weights = jnp.exp(mul(kh, qh, 0, 0) + bias[...])
        inv = 1.0 / jnp.sum(weights, axis=0, keepdims=True)
        attn = (mul(vh, weights.astype(BF16), 1, 0) * inv).astype(BF16)
        attn_t[part, :] = attn
        correction = jnp.sum(ga * attn.astype(F32), axis=0, keepdims=True) * inv
        stats[h : h + 1, :] = inv
        stats[HEADS + h : HEADS + h + 1, :] = correction
        dots = mul(vh, (ga * inv).astype(BF16), 0, 0)
        slopes = (weights * (dots - correction)).astype(BF16)
        dq_f[part, :] = mul(kh, slopes, 1, 0) * SCALE
        if h % 2 == 1:
            advance_if(4)
        if h % 3 == 2 and pending:
            step = pending.pop(0)
            line_recv(step - 1, (1,))
            line_send(step, (1,))
    for step in pending:
        line_recv(step - 1, (1,))
        line_send(step, (1,))
    for k in range(1, nb):
        to = lax.rem(me + k, nb)
        remote(stats, all_stats.at[me], ssend.at[k], srecv.at[k], "blk", to).start()
    all_stats[me] = stats[...]
    dq = head_norm_pull(queries, q_scaling, dq_f[...]).astype(BF16)
    terms[3] = mul(attn_t[...], gout[...], 1, 0).astype(BF16)
    begin(3)
    terms[0] = mul(normed, dq, 0, 1).astype(BF16)
    begin(0)
    out = x + mul(mean_rows[...], wm[...], 1, 0) + mul(attn_t[...], wo[...], 0, 0)
    layer[...] = out.astype(BF16)
    for k in range(1, nd):
        swap(sback, rback, bsend, brecv, k, True).wait_recv()
    halo = mul(onehot[...], rback[...].reshape(nd * cap, width), 1, 0)

    own_keys, k_scaling = head_norm(mul(wk[...], normed, 0, 1))
    k_own = own_keys.reshape(width, rows).astype(BF16)
    v_own = mul(wv[...], normed, 0, 1).astype(BF16)
    line_recv(nb - 2, (1,))
    for k in range(1, nb):
        to = lax.rem(me + k, nb)
        origin = lax.rem(me + nb - k, nb)
        remote(stats, all_stats.at[origin], ssend.at[k], srecv.at[k], "blk", to).wait()
    inv_all = jnp.concatenate([all_stats[b, :HEADS, :] for b in range(nb)], axis=1)
    corrections = jnp.concatenate([all_stats[b, HEADS:, :] for b in range(nb)], axis=1)
    ga_all = mul(wo[...], gouts[...].reshape(nb * rows, width), 1, 1)
    ga_all = ga_all.reshape(HEADS, HEAD_DIM, nb * rows) * inv_all[:, None, :]
    gh_t[...] = ga_all.reshape(gh_t.shape).astype(BF16)
    advance_if(4)
    for h in range(HEADS):
        part = slice(h * HEAD_DIM, (h + 1) * HEAD_DIM)
        kh, vh, qh, gh = k_own[part, :], v_own[part, :], q_t[part, :], gh_t[part, :]
        weights = jnp.exp(mul(kh, qh, 0, 0) + bias_own[...])
        dots = mul(vh, gh, 0, 0)
        slopes = (weights * (dots - corrections[h : h + 1, :])).astype(BF16)
        dk_f[part, :] = mul(qh, slopes, 1, 1)
        dv_f[part, :] = mul(gh, weights.astype(BF16), 1, 1)
        if h % 2 == 0:
            advance_if(4)
        else:
            advance_if(3)
            advance_if(0)
    dk = head_norm_pull(own_keys, k_scaling, dk_f[...]).astype(BF16)
    dv = dv_f[...].astype(BF16)
    terms[1] = mul(normed, dk, 0, 1).astype(BF16)
    begin(1)
    terms[2] = mul(normed, dv, 0, 1).astype(BF16)
    begin(2)
    for p in (4, 3, 0):
        advance_if(p)
    dnormed = (mul(wq[...], dq, 1, 0) + mul(wk[...], dk, 1, 0) + mul(wv[...], dv, 1, 0)).T
    dnormed = dnormed + halo
    xs = x * scaling
    gacc[0] = jnp.broadcast_to(jnp.sum(dnormed * xs, axis=0, keepdims=True), gacc.shape[1:])
    gain_copy(0).start()
    dscaled = dnormed * gain[...]
    dx = scaling * (dscaled - xs * jnp.mean(dscaled * xs, axis=-1, keepdims=True))
    fgrad[...] = (gout[...].astype(F32) + dx).astype(BF16)
    turn = 0
    while any(stage[p] < 2 * n for p in range(PIECES)):
        for p in (1, 2, 3, 0, 4):
            advance_if(p)
        if turn < n:
            gain_copy(turn).wait()
            gacc[turn + 1] = gacc[turn] + grecv[turn]
            if turn + 1 < n:
                gain_copy(turn + 1).start()
        turn += 1
    gsum[...] = gacc[n]

    for p in range(PIECES):
        settle(p)
    for step in range(nb - 1):
        line_send(step, (0, 1, 2), False)
    for k in range(1, nd):
        swap(sbuf, rbuf, asend, arecv, k, False).wait_send()
        swap(sback, rback, bsend, brecv, k, False).wait_send()


def layer_call(nd, nb, *args):
    feat, sidx = args[0], args[9]
    rows, width = feat.shape
    cap = sidx.shape[1]
    total, slots = nb * rows, nd * cap
    vmem = pl.BlockSpec(memory_space=pltpu.VMEM)
    smem = pl.BlockSpec(memory_space=pltpu.SMEM)
    dma = pltpu.SemaphoreType.DMA
    V = pltpu.VMEM
    n = len(plan(nd, nb, width, False))
    buffers = []
    for flip in FLIPS:
        for _, _, count, _ in plan(nd, nb, width, flip):
            buffers += [V((count, width), BF16)] * 2
    return pl.pallas_call(
        partial(layer_kernel, nd, nb),
        out_shape=[
            jax.ShapeDtypeStruct((rows, width), BF16),
            jax.ShapeDtypeStruct((rows, width), BF16),
            jax.ShapeDtypeStruct((PIECES * width, width), BF16),
            jax.ShapeDtypeStruct((8, width), F32),
        ],
        in_specs=[vmem] * 12 + [smem] * 2,
        out_specs=[vmem] * 4,
        scratch_shapes=[
            V((nb, rows, width), BF16), V((nb, rows, width), BF16),
            V((nb, 16, rows), jnp.int32), V((16, rows), jnp.int32),
            V((nd, cap, width), BF16), V((nd, cap, width), BF16),
            V((nd, cap, width), BF16), V((nd, cap, width), BF16),
            V((rows, slots), F32), V((rows, slots), BF16),
            V((width, total), BF16), V((width, total), BF16), V((width, total), BF16),
            V((width, rows), BF16), V((width, rows), F32), V((width, rows), BF16),
            V((rows, width), BF16),
            V((total, rows), F32), V((rows, total), F32),
            V((width, rows), F32), V((width, rows), F32), V((width, rows), F32),
            V((width, total), BF16),
            V((2 * HEADS, rows), F32), V((nb, 2 * HEADS, rows), F32),
            V((PIECES, width, width), BF16),
            V((n + 1, 8, width), F32), V((n, 8, width), F32),
            dma((2, nb, 3)), dma((2, nb, 3)),
            dma((nd,)), dma((nd,)), dma((nd,)), dma((nd,)), dma((nb,)), dma((nb,)),
            dma((PIECES, n)), dma((PIECES, n)), dma((n,)), dma((n,)),
            dma((PIECES, n)), dma((PIECES, n)),
        ]
        + buffers,
        compiler_params=params(0),
    )(*args)


def local(
    node_features, norm_gain, w_query, w_key, w_value, w_out, w_message, node_cluster,
    block_pattern, send_rows, send_counts, edge_src, edge_dst, out_grad,
):
    rows, width = node_features.shape
    nd = lax.axis_size("dom")
    nb = lax.axis_size("blk")
    layer_out, feature_grad, sums, gain_sum = layer_call(
        nd, nb, node_features, out_grad, norm_gain.reshape(1, width),
        w_query, w_key, w_value, w_out, w_message, node_cluster.reshape(1, rows), send_rows,
        edge_src.reshape(1, -1), edge_dst.reshape(1, -1), send_counts, block_pattern,
    )
    weight_sums = sums.reshape(PIECES, width, width).astype(F32)
    return (layer_out, feature_grad, weight_sums, gain_sum[0])


def solution(mesh):
    nodes = P(("dom", "blk"))
    wide = P(("dom", "blk"), None)
    placed = (
        wide, P(), P(), P(), P(), P(), P(), nodes, wide, wide, nodes, nodes, nodes, wide,
    )
    return jax.shard_map(
        local,
        mesh=mesh,
        in_specs=placed,
        out_specs=(wide, wide, P(), P()),
        check_vma=False,
    )
```

time: 157 us -> 116 us (0.74)
  Pallas kernels: 139 us -> 108 us
  local copies, waits for them, and re-layouts: 9.14 us -> 2.77 us
  other arithmetic: 8.1 us -> 4.82 us
    pallas_call x5 -> x1, Pallas kernels: 139 us -> 108 us  [layer_call(): pl.pallas_call(partial(layer_kernel, nd, nb), out_shape=[jax.ShapeDtypeSt...]
    convert_element_type x0 -> x1, other arithmetic: none -> 4.82 us  [local(): weight_sums = sums.reshape(PIECES, width, width).astype(F32)]
    concatenate x2 -> x0, other arithmetic: 4.39 us -> none  [the longest x1 3.03 us: local(): weight_sums = jnp.concatenate([sums[0], sums[1]], axis=-1)]
    reshape x3 -> x0, local copies, waits for them, and re-layouts: 4.12 us -> none  [the longest x1 1.48 us: local(): node_cluster.reshape(rows, 1)]
    slice x2 -> x0, local copies, waits for them, and re-layouts: 2.96 us -> none  [the longest x1 2.12 us: local(): weight_sums = jnp.concatenate([sums[0], sums[1]], axis=-1)]
    select_n x3 -> x0, other arithmetic: 2.82 us -> none  [the longest x1 1.35 us: local(): sidx = jnp.where(live, send_rows, -1)]
where the time goes in v2:
time: 116 us
  Pallas kernels  108 us (93%)
  other arithmetic  4.82 us (4%)
  local copies, waits for them, and re-layouts  2.77 us (2%)
    pallas_call x1, Pallas kernels, layer_call(): pl.pallas_call(partial(layer_kernel, nd, nb), out_shape=[jax.ShapeDtypeSt...  108 us
    convert_element_type x1, other arithmetic, local(): weight_sums = sums.reshape(PIECES, width, width).astype(F32)  4.82 us

profile of v2, /device:TPU:0, one launch (start us, length us, event | category | flops | bytes accessed | tf_op | source)
XLA Modules:
  0.0 115.9 jit_solution(18235206504552093456)
XLA Ops:
  0.6 107.7 %shard_map.165 = (bf16[256,512]{1,0:T(8,128)(2,1)}, bf16[256,512]{1,0:T(8,128)(2,1)}, bf16[2560,512]{1,0:T(8,128)(2,1)}, f32[8,512]{1,0:T(8,128)}) custom-call(bf16[256,512]{1,0:T(8,128)(2,1)} %feat.1, bf16[256,512]{1,0:T(8,128)(2,1)} %gout.1, f32[1,512]{1,0:T(1,128)} %bitcast.10, bf16[512,512]{1,0:T(8,128)(2,1)} %wq.1, bf16[512,512]{1,0:T(8,128)(2,1)} %wk.1, ...), custom_call_target="tpu_custom_call" | custom-call | tf_op jit(solution)/shard_map/pallas_call | solution.py:414
  108.3 0.0 copy-start.1
  108.3 0.0 copy-start
  108.4 1.4 %slice.3 = f32[1,512]{1,0:T(1,128)} slice(f32[8,512]{1,0:T(8,128)} %get-tuple-element.11), slice={[0:1], [0:512]} | slice | bytes 4096 | tf_op jit(solution)/shard_map/slice | solution.py:462
  109.7 4.8 %convert.1 = f32[5,512,512]{2,1,0:T(8,128)} convert(bf16[5,512,512]{2,1,0:T(8,128)(2,1)} %bitcast.7) | non-fusion elementwise | flops 1310720 | bytes 7864320 | tf_op jit(solution)/shard_map/convert_element_type | solution.py:461
  114.5 0.0 copy-done.1
  114.5 0.7 copy.20
  115.2 0.0 copy-done
  115.2 0.7 copy.21
Async XLA Ops:
  108.3 6.2 %copy-start.1 = (bf16[256,512]{1,0:T(8,128)(2,1)S(1)}, bf16[256,512]{1,0:T(8,128)(2,1)}, u32[]{:S(2)}) copy-start(bf16[256,512]{1,0:T(8,128)(2,1)} %get-tuple-element.16) | copy-start | bytes 786436
  108.3 6.9 %copy-start = (bf16[256,512]{1,0:T(8,128)(2,1)S(1)}, bf16[256,512]{1,0:T(8,128)(2,1)}, u32[]{:S(2)}) copy-start(bf16[256,512]{1,0:T(8,128)(2,1)} %get-tuple-element.17) | copy-start | bytes 786436

commit v3 on v2

--- a/solution.py
+++ b/solution.py
@@ -54,17 +54,20 @@
     )
 
 
-def plan(nd, nb, rows, flip):
-    dom_bits = [1 << i for i in range(nd.bit_length() - 1)]
-    blk_bits = [1 << i for i in range(nb.bit_length() - 1)]
+def plan(nd, rows, flip):
+    bits = [1 << i for i in range(nd.bit_length() - 1)]
     if flip:
-        dom_bits = dom_bits[:1] + dom_bits[:0:-1]
+        bits = bits[:1] + bits[:0:-1]
     steps = []
-    for axis, bit in [("dom", b) for b in dom_bits] + [("blk", b) for b in blk_bits]:
+    for bit in bits:
         halves = rows % 32 == 0
         rows = rows // 2 if halves else rows
-        steps.append((axis, bit, rows, halves))
+        steps.append((bit, rows, halves))
     return steps
+
+
+def line_rows(nb, rows):
+    return rows // nb if rows % (16 * nb) == 0 else rows
 
 
 FLIPS = (True, False, True, False, True)
@@ -76,10 +79,11 @@
     feat, gout, gain, wq, wk, wv, wo, wm, labels, sidx, esrc, edst, live_counts, pattern,
     layer, fgrad, sums, gsum,
     feats, gouts, metas, mine, sbuf, rbuf, sback, rback, cnt, onehot,
-    k_t, v_t, q_t, q_own, ga_t, attn_t, mean_rows, bias, bias_own, dq_f, dk_f, dv_f, gh_t,
+    k_t, v_t, q_t, q_own, ga_t, attn_t, mean_rows, bias, bias_own, dq_f, dk_f, dv_f, gh_t, k_own_t, v_own_t,
     stats, all_stats, terms, gacc, grecv,
     zsend, zrecv, asend, arecv, bsend, brecv, ssend, srecv,
-    rsend, rrecv, gsend, grsem, hsend, hrecv,
+    rsend, rrecv, gsend, grsem, hsend, hrecv, lsend, lrecv, tsend, trecv, usend, urecv, gline,
+    w_all, num, den,
     *buffers,
 ):
     me = lax.axis_index("blk")
@@ -87,9 +91,13 @@
     index = {"dom": my_dom, "blk": me}
     rows, width = feat.shape
     cap = sidx.shape[1]
-    plans = [plan(nd, nb, width, f) for f in FLIPS]
+    plans = [plan(nd, width, f) for f in FLIPS]
     n = len(plans[0])
     acc = [[buffers[2 * (p * n + s)] for s in range(n)] for p in range(PIECES)]
+    last = plans[0][-1][1]
+    share = line_rows(nb, last)
+    stages = 2 * n + 2 if share < last else 2 * n + 1
+    gline_in = buffers[-PIECES:]
     got = [[buffers[2 * (p * n + s) + 1] for s in range(n)] for p in range(PIECES)]
 
     barrier = pltpu.get_barrier_semaphore()
@@ -161,64 +169,135 @@
         return mine_bit, index[axis] + bit - 2 * bit * mine_bit
 
     def gain_copy(s):
-        axis, bit, _, _ = plans[1][s]
-        return remote(gacc.at[s], grecv.at[s], gsend.at[s], grsem.at[s], axis, peer_of(axis, bit)[1])
+        bit, _, _ = plans[1][s]
+        return remote(
+            gacc.at[s], grecv.at[s], gsend.at[s], grsem.at[s], "dom", peer_of("dom", bit)[1]
+        )
+
+    def gain_line(k, incoming):
+        to = lax.rem(me + k, nb)
+        origin = lax.rem(me + nb - k, nb)
+        return remote(
+            gacc.at[n], gline.at[origin if incoming else me], usend.at[k], urecv.at[k], "blk", to
+        )
+
+    def gain_turn(turn):
+        if turn < n:
+            gain_copy(turn).wait()
+            gacc[turn + 1] = gacc[turn] + grecv[turn]
+            if turn + 1 < n:
+                gain_copy(turn + 1).start()
+            else:
+                for k in range(1, nb):
+                    gain_line(k, False).start()
+                gline[me] = gacc[n]
+        elif turn == n:
+            for k in range(1, nb):
+                gain_line(k, True).wait()
+            total = gline[0]
+            for b in range(1, nb):
+                total = total + gline[b]
+            gsum[...] = total[0:1, :]
 
     def reduce_copy(p, s):
-        axis, bit, count, halves = plans[p][s]
-        bit_set, peer = peer_of(axis, bit)
+        bit, count, halves = plans[p][s]
+        bit_set, peer = peer_of("dom", bit)
         src = terms.at[p] if s == 0 else acc[p][s - 1]
         away = (1 - bit_set) * count if halves else 0
         keep = bit_set * count if halves else 0
         c = remote(
-            src.at[aligned(away, count), :], got[p][s], rsend.at[p, s], rrecv.at[p, s], axis, peer
+            src.at[aligned(away, count), :], got[p][s], rsend.at[p, s], rrecv.at[p, s], "dom", peer
         )
         return c, src, keep
 
+    def share_of(b):
+        return aligned(b * share, share) if share < last else aligned(0, last)
+
+    def line_reduce(p, k, incoming):
+        to = lax.rem(me + k, nb)
+        origin = lax.rem(me + nb - k, nb)
+        return remote(
+            acc[p][n - 1].at[share_of(to), :],
+            gline_in[p].at[origin if incoming else me],
+            lsend.at[p, k], lrecv.at[p, k], "blk", to,
+        )
+
+    def line_spread(p, k, incoming):
+        to = lax.rem(me + k, nb)
+        origin = lax.rem(me + nb - k, nb)
+        src = sums.at[aligned(p * width + first[p] + me * share, share), :]
+        dst = sums.at[aligned(p * width + first[p] + (origin if incoming else me) * share, share), :]
+        return remote(src, dst, tsend.at[p, k], trecv.at[p, k], "blk", to)
+
     def spread_copy(p, s):
-        axis, peer, start, count = history[p][s]
+        peer, start, count = history[p][s]
         place = sums.at[aligned(p * width + start, count), :]
-        return remote(place, place, hsend.at[p, s], hrecv.at[p, s], axis, peer)
+        return remote(place, place, hsend.at[p, s], hrecv.at[p, s], "dom", peer)
+
+    def back_step(p, stage_now):
+        return stages - 1 - stage_now
+
+    def launch(p):
+        s = stage[p]
+        if s < n:
+            reduce_copy(p, s)[0].start()
+        elif s == n:
+            for k in range(1, nb):
+                line_reduce(p, k, False).start()
+            gline_in[p][me] = acc[p][n - 1][share_of(me), :]
+        elif s < stages - n:
+            for k in range(1, nb):
+                line_spread(p, k, False).start()
+        elif s < stages:
+            spread_copy(p, back_step(p, s)).start()
 
     def begin(p):
         stage[p] = 0
         first[p] = 0
-        reduce_copy(p, 0)[0].start()
+        launch(p)
 
     def advance(p):
         s = stage[p]
         if s < n:
             c, src, keep = reduce_copy(p, s)
-            axis, bit, count, halves = plans[p][s]
+            bit, count, halves = plans[p][s]
             c.wait_recv()
-            total = (
-                src[aligned(keep, count), :].astype(F32) + got[p][s][...].astype(F32)
-            ).astype(BF16)
+            total = src[aligned(keep, count), :].astype(F32) + got[p][s][...].astype(F32)
             first[p] = first[p] + keep
-            history[p].append((axis, peer_of(axis, bit)[1], first[p], count))
-            if s == n - 1:
-                sums[aligned(p * width + first[p], count), :] = total
-            else:
-                acc[p][s][...] = total
-                reduce_copy(p, s + 1)[0].start()
+            history[p].append((peer_of("dom", bit)[1], first[p], count))
+            acc[p][s][...] = total.astype(BF16)
+        elif s == n:
+            for k in range(1, nb):
+                line_reduce(p, k, True).wait_recv()
+            total = gline_in[p][0].astype(F32)
+            for b in range(1, nb):
+                total = total + gline_in[p][b].astype(F32)
+            mine_at = me * share if share < last else 0
+            sums[aligned(p * width + first[p] + mine_at, share), :] = total.astype(BF16)
+        elif s < stages - n:
+            for k in range(1, nb):
+                line_spread(p, k, True).wait_recv()
         else:
-            spread_copy(p, 2 * n - 1 - s).wait_recv()
+            spread_copy(p, back_step(p, s)).wait_recv()
         s += 1
-        while n <= s < 2 * n and not plans[p][2 * n - 1 - s][3]:
+        while stages - n <= s < stages and not plans[p][back_step(p, s)][2]:
             s += 1
         stage[p] = s
-        if n <= s < 2 * n:
-            spread_copy(p, 2 * n - 1 - s).start()
+        launch(p)
 
     def advance_if(p):
-        if 0 <= stage[p] < 2 * n:
+        if 0 <= stage[p] < stages:
             advance(p)
 
     def settle(p):
         for s in range(n):
             reduce_copy(p, s)[0].wait_send()
-            if plans[p][s][3]:
+            if plans[p][s][2]:
                 spread_copy(p, s).wait_send()
+        for k in range(1, nb):
+            line_reduce(p, k, False).wait_send()
+            if share < last:
+                line_spread(p, k, False).wait_send()
 
     line_send(0, (0, 2))
     feats[me] = feat[...]
@@ -264,9 +343,56 @@
         swap(sback, rback, bsend, brecv, k, False).start()
     rback[my_dom] = sback[my_dom]
 
+    own_row = own_labels.astype(F32)
+    own_column = jnp.broadcast_to(own_row, (rows, rows)).T
     queries, q_scaling = head_norm(mul(wq[...], normed, 0, 1))
     q_own[...] = (queries * SCALE).reshape(q_own.shape).astype(BF16)
     ga_t[...] = mul(wo[...], gout[...], 1, 1)
+    num[...] = jnp.zeros_like(num)
+    den[...] = jnp.zeros_like(den)
+
+    def heads(body):
+        def pair(i, carry):
+            for j in range(2):
+                h = 2 * i + j
+                body(h, pl.ds(pl.multiple_of(h * HEAD_DIM, HEAD_DIM), HEAD_DIM))
+            return carry
+
+        lax.fori_loop(0, HEADS // 2, pair, 0)
+
+    def forward(block):
+        at = pl.ds(pl.multiple_of(block * rows, rows), rows)
+        xb = feats[block].astype(F32)
+        nb_rows = (xb * row_scale(xb) * gain[...]).astype(BF16)
+        keys, _ = head_norm(mul(wk[...], nb_rows, 0, 1))
+        k_t[:, at] = keys.reshape(width, rows).astype(BF16)
+        v_t[:, at] = mul(wv[...], nb_rows, 0, 1).astype(BF16)
+        block_queries, _ = head_norm(mul(wq[...], nb_rows, 0, 1))
+        q_t[:, at] = (block_queries * SCALE).reshape(width, rows).astype(BF16)
+        column = jnp.broadcast_to(metas[block, 0:1, :].astype(F32), (rows, rows)).T
+        seen = jnp.where(pattern[0, block] == 1, own_row, -1.0)
+        bias[...] = jnp.where(column == seen, -SHIFT, MASKED)
+        towards = metas[block, pl.ds(1 + me, 1), :].astype(F32)
+        bias_own[:, at] = jnp.where(own_column == towards, -SHIFT, MASKED)
+
+        def one(h, part):
+            weights = jnp.exp(mul(k_t[part, at], q_own[part, :], 0, 0) + bias[...])
+            den[pl.ds(h, 1), :] += jnp.sum(weights, axis=0, keepdims=True)
+            weights = weights.astype(BF16)
+            w_all[h, at, :] = weights
+            num[part, :] += mul(v_t[part, at], weights, 1, 0)
+
+        heads(one)
+
+    def at_distance(distance, body):
+        for way in range(2):
+            block = me - distance if way == 0 else me + distance
+
+            @pl.when(block >= 0 if way == 0 else block < nb)
+            def _():
+                body(block)
+
+    forward(me)
     for k in range(1, nd):
         swap(sbuf, rbuf, asend, arecv, k, True).wait_recv()
     mean = (mul(counts, rbuf[...].reshape(nd * cap, width), 1, 0) / degree).astype(BF16)
@@ -276,38 +402,26 @@
     for step in range(2, nb - 1):
         line_recv(step - 1, (0, 2))
         line_send(step, (0, 2))
+        at_distance(step - 1, forward)
+        advance_if(4)
     line_recv(nb - 2, (0, 2))
     line_send(0, (1,))
-
-    x_all = feats[...].reshape(nb * rows, width).astype(F32)
-    normed_all = (x_all * row_scale(x_all) * gain[...]).astype(BF16)
-    keys, _ = head_norm(mul(wk[...], normed_all, 0, 1))
-    k_t[...] = keys.reshape(k_t.shape).astype(BF16)
-    v_t[...] = mul(wv[...], normed_all, 0, 1).astype(BF16)
-    all_queries, _ = head_norm(mul(wq[...], normed_all, 0, 1))
-    q_t[...] = (all_queries * SCALE).reshape(q_t.shape).astype(BF16)
-    own_row = own_labels.astype(F32)
-    own_column = jnp.broadcast_to(own_row, (rows, rows)).T
-    for b in range(nb):
-        at = slice(b * rows, (b + 1) * rows)
-        row = jnp.where(pattern[0, b] == 1, metas[b, 0:1, :], -1).astype(F32)
-        column = jnp.broadcast_to(row, (rows, rows)).T
-        bias[at, :] = jnp.where(column == own_row, -SHIFT, MASKED)
-        towards = metas[b, pl.ds(1 + me, 1), :].astype(F32)
-        bias_own[:, at] = jnp.where(own_column == towards, -SHIFT, MASKED)
+    for distance in range(max(nb - 2, 1), nb):
+        at_distance(distance, forward)
+        advance_if(4)
+
     pending = list(range(1, nb - 1))
     for h in range(HEADS):
         part = slice(h * HEAD_DIM, (h + 1) * HEAD_DIM)
-        kh, vh, qh, ga = k_t[part, :], v_t[part, :], q_own[part, :], ga_t[part, :]
-        weights = jnp.exp(mul(kh, qh, 0, 0) + bias[...])
-        inv = 1.0 / jnp.sum(weights, axis=0, keepdims=True)
-        attn = (mul(vh, weights.astype(BF16), 1, 0) * inv).astype(BF16)
+        kh, vh, ga = k_t[part, :], v_t[part, :], ga_t[part, :]
+        inv = 1.0 / den[h : h + 1, :]
+        attn = (num[part, :] * inv).astype(BF16)
         attn_t[part, :] = attn
         correction = jnp.sum(ga * attn.astype(F32), axis=0, keepdims=True) * inv
         stats[h : h + 1, :] = inv
         stats[HEADS + h : HEADS + h + 1, :] = correction
         dots = mul(vh, (ga * inv).astype(BF16), 0, 0)
-        slopes = (weights * (dots - correction)).astype(BF16)
+        slopes = (w_all[h].astype(F32) * (dots - correction)).astype(BF16)
         dq_f[part, :] = mul(kh, slopes, 1, 0) * SCALE
         if h % 2 == 1:
             advance_if(4)
@@ -336,36 +450,49 @@
     own_keys, k_scaling = head_norm(mul(wk[...], normed, 0, 1))
     k_own = own_keys.reshape(width, rows).astype(BF16)
     v_own = mul(wv[...], normed, 0, 1).astype(BF16)
-    line_recv(nb - 2, (1,))
+    k_own_t[...] = k_own
+    v_own_t[...] = v_own
+    dk_f[...] = jnp.zeros_like(dk_f)
+    dv_f[...] = jnp.zeros_like(dv_f)
+
+    def backward(block):
+        at = pl.ds(pl.multiple_of(block * rows, rows), rows)
+        ga_b = mul(wo[...], gouts[block], 1, 1).reshape(HEADS, HEAD_DIM, rows)
+        inv_b = all_stats[block, :HEADS, :]
+        gh_t[...] = (ga_b * inv_b[:, None, :]).reshape(width, rows).astype(BF16)
+
+        def one(h, part):
+            qh, gh = q_t[part, at], gh_t[part, :]
+            weights = jnp.exp(mul(k_own_t[part, :], qh, 0, 0) + bias_own[:, at])
+            dots = mul(v_own_t[part, :], gh, 0, 0)
+            correction = all_stats[block, pl.ds(HEADS + h, 1), :]
+            slopes = (weights * (dots - correction)).astype(BF16)
+            dk_f[part, :] += mul(qh, slopes, 1, 1)
+            dv_f[part, :] += mul(gh, weights.astype(BF16), 1, 1)
+
+        heads(one)
+
+    backward(me)
+    for p in (4, 3, 0):
+        advance_if(p)
     for k in range(1, nb):
         to = lax.rem(me + k, nb)
         origin = lax.rem(me + nb - k, nb)
         remote(stats, all_stats.at[origin], ssend.at[k], srecv.at[k], "blk", to).wait()
-    inv_all = jnp.concatenate([all_stats[b, :HEADS, :] for b in range(nb)], axis=1)
-    corrections = jnp.concatenate([all_stats[b, HEADS:, :] for b in range(nb)], axis=1)
-    ga_all = mul(wo[...], gouts[...].reshape(nb * rows, width), 1, 1)
-    ga_all = ga_all.reshape(HEADS, HEAD_DIM, nb * rows) * inv_all[:, None, :]
-    gh_t[...] = ga_all.reshape(gh_t.shape).astype(BF16)
-    advance_if(4)
-    for h in range(HEADS):
-        part = slice(h * HEAD_DIM, (h + 1) * HEAD_DIM)
-        kh, vh, qh, gh = k_own[part, :], v_own[part, :], q_t[part, :], gh_t[part, :]
-        weights = jnp.exp(mul(kh, qh, 0, 0) + bias_own[...])
-        dots = mul(vh, gh, 0, 0)
-        slopes = (weights * (dots - corrections[h : h + 1, :])).astype(BF16)
-        dk_f[part, :] = mul(qh, slopes, 1, 1)
-        dv_f[part, :] = mul(gh, weights.astype(BF16), 1, 1)
-        if h % 2 == 0:
-            advance_if(4)
-        else:
-            advance_if(3)
-            advance_if(0)
+    for distance in range(1, nb - 1):
+        at_distance(distance, backward)
+        for p in (4, 3, 0):
+            advance_if(p)
+    line_recv(nb - 2, (1,))
+    at_distance(nb - 1, backward)
+    for p in (4, 3, 0):
+        advance_if(p)
     dk = head_norm_pull(own_keys, k_scaling, dk_f[...]).astype(BF16)
     dv = dv_f[...].astype(BF16)
+    terms[2] = mul(normed, dv, 0, 1).astype(BF16)
+    begin(2)
     terms[1] = mul(normed, dk, 0, 1).astype(BF16)
     begin(1)
-    terms[2] = mul(normed, dv, 0, 1).astype(BF16)
-    begin(2)
     for p in (4, 3, 0):
         advance_if(p)
     dnormed = (mul(wq[...], dq, 1, 0) + mul(wk[...], dk, 1, 0) + mul(wv[...], dv, 1, 0)).T
@@ -377,16 +504,11 @@
     dx = scaling * (dscaled - xs * jnp.mean(dscaled * xs, axis=-1, keepdims=True))
     fgrad[...] = (gout[...].astype(F32) + dx).astype(BF16)
     turn = 0
-    while any(stage[p] < 2 * n for p in range(PIECES)):
-        for p in (1, 2, 3, 0, 4):
+    while any(stage[p] < stages for p in range(PIECES)) or turn <= n:
+        for p in (2, 1, 3, 0, 4):
             advance_if(p)
-        if turn < n:
-            gain_copy(turn).wait()
-            gacc[turn + 1] = gacc[turn] + grecv[turn]
-            if turn + 1 < n:
-                gain_copy(turn + 1).start()
+        gain_turn(turn)
         turn += 1
-    gsum[...] = gacc[n]
 
     for p in range(PIECES):
         settle(p)
@@ -406,10 +528,12 @@
     smem = pl.BlockSpec(memory_space=pltpu.SMEM)
     dma = pltpu.SemaphoreType.DMA
     V = pltpu.VMEM
-    n = len(plan(nd, nb, width, False))
+    n = len(plan(nd, width, False))
+    last = plan(nd, width, False)[-1][1]
+    lines = [V((nb, line_rows(nb, last), width), BF16)] * PIECES
     buffers = []
     for flip in FLIPS:
-        for _, _, count, _ in plan(nd, nb, width, flip):
+        for _, count, _ in plan(nd, width, flip):
             buffers += [V((count, width), BF16)] * 2
     return pl.pallas_call(
         partial(layer_kernel, nd, nb),
@@ -417,7 +541,7 @@
             jax.ShapeDtypeStruct((rows, width), BF16),
             jax.ShapeDtypeStruct((rows, width), BF16),
             jax.ShapeDtypeStruct((PIECES * width, width), BF16),
-            jax.ShapeDtypeStruct((8, width), F32),
+            jax.ShapeDtypeStruct((1, width), F32),
         ],
         in_specs=[vmem] * 12 + [smem] * 2,
         out_specs=[vmem] * 4,
@@ -430,9 +554,9 @@
             V((width, total), BF16), V((width, total), BF16), V((width, total), BF16),
             V((width, rows), BF16), V((width, rows), F32), V((width, rows), BF16),
             V((rows, width), BF16),
-            V((total, rows), F32), V((rows, total), F32),
+            V((rows, rows), F32), V((rows, total), F32),
             V((width, rows), F32), V((width, rows), F32), V((width, rows), F32),
-            V((width, total), BF16),
+            V((width, rows), BF16), V((width, rows), BF16), V((width, rows), BF16),
             V((2 * HEADS, rows), F32), V((nb, 2 * HEADS, rows), F32),
             V((PIECES, width, width), BF16),
             V((n + 1, 8, width), F32), V((n, 8, width), F32),
@@ -440,10 +564,31 @@
             dma((nd,)), dma((nd,)), dma((nd,)), dma((nd,)), dma((nb,)), dma((nb,)),
             dma((PIECES, n)), dma((PIECES, n)), dma((n,)), dma((n,)),
             dma((PIECES, n)), dma((PIECES, n)),
+            dma((PIECES, nb)), dma((PIECES, nb)), dma((PIECES, nb)), dma((PIECES, nb)),
+            dma((nb,)), dma((nb,)),
+            V((nb, 8, width), F32),
+            V((HEADS, total, rows), BF16), V((width, rows), F32), V((HEADS, rows), F32),
         ]
-        + buffers,
+        + buffers
+        + lines,
         compiler_params=params(0),
     )(*args)
+
+
+def widen_kernel(x, out):
+    out[0] = x[...].astype(F32)
+
+
+def widen(sums):
+    width = sums.shape[1]
+    return pl.pallas_call(
+        widen_kernel,
+        grid=(PIECES,),
+        out_shape=jax.ShapeDtypeStruct((PIECES, width, width), F32),
+        in_specs=[pl.BlockSpec((width, width), lambda i: (i, 0))],
+        out_specs=pl.BlockSpec((1, width, width), lambda i: (i, 0, 0)),
+        compiler_params=params(),
+    )(sums)
 
 
 def local(
@@ -458,8 +603,7 @@
         w_query, w_key, w_value, w_out, w_message, node_cluster.reshape(1, rows), send_rows,
         edge_src.reshape(1, -1), edge_dst.reshape(1, -1), send_counts, block_pattern,
     )
-    weight_sums = sums.reshape(PIECES, width, width).astype(F32)
-    return (layer_out, feature_grad, weight_sums, gain_sum[0])
+    return (layer_out, feature_grad, widen(sums), gain_sum.reshape(width))
 
 
 def solution(mesh):

time: 116 us -> 115 us (level)
  other arithmetic: 4.82 us -> 0 us
  Pallas kernels: 108 us -> 112 us
    pallas_call x0 -> x1, Pallas kernels: none -> 5.2 us  [widen(): pl.pallas_call(widen_kernel, grid=(PIECES,), out_shape=jax.ShapeDtypeStru...]
    convert_element_type x1 -> x0, other arithmetic: 4.82 us -> none  [local(): weight_sums = sums.reshape(PIECES, width, width).astype(F32)]
    slice x1 -> x0, local copies, waits for them, and re-layouts: 1.35 us -> none  [local(): return (layer_out, feature_grad, weight_sums, gain_sum[0])]
where the time goes in v3:
time: 115 us
  Pallas kernels  112 us (97%)
  local copies, waits for them, and re-layouts  2 us (2%)
    pallas_call x1, Pallas kernels, layer_call(): pl.pallas_call(partial(layer_kernel, nd, nb), out_shape=[jax.ShapeDtypeSt...  107 us
    pallas_call x1, Pallas kernels, widen(): pl.pallas_call(widen_kernel, grid=(PIECES,), out_shape=jax.ShapeDtypeStru...  5.2 us

profile of v3, /device:TPU:0, one launch (start us, length us, event | category | flops | bytes accessed | tf_op | source)
XLA Modules:
  0.0 114.6 jit_solution(637865492255080260)
XLA Ops:
  0.6 106.7 %shard_map.165 = (bf16[256,512]{1,0:T(8,128)(2,1)}, bf16[256,512]{1,0:T(8,128)(2,1)}, bf16[2560,512]{1,0:T(8,128)(2,1)}, f32[1,512]{1,0:T(1,128)}) custom-call(bf16[256,512]{1,0:T(8,128)(2,1)} %feat.1, bf16[256,512]{1,0:T(8,128)(2,1)} %gout.1, f32[1,512]{1,0:T(1,128)} %bitcast.7, bf16[512,512]{1,0:T(8,128)(2,1)} %wq.1, bf16[512,512]{1,0:T(8,128)(2,1)} %wk.1, ...), custom_call_target="tpu_custom_call" | custom-call | tf_op jit(solution)/shard_map/pallas_call | solution.py:538
  107.3 0.0 copy-start.1
  107.4 0.0 copy-start
  107.4 0.0 copy-start.2
  107.4 5.2 %shard_map.166 = f32[5,512,512]{2,1,0:T(8,128)} custom-call(bf16[2560,512]{1,0:T(8,128)(2,1)} %get-tuple-element.10.x), custom_call_target="tpu_custom_call" | custom-call | tf_op jit(solution)/shard_map/pallas_call | solution.py:584
  112.6 0.0 copy-done.1
  112.6 0.7 copy.21
  113.3 0.0 copy-done
  113.3 0.7 copy.22
  114.0 0.0 copy-done.2
  114.0 0.6 copy.23
Async XLA Ops:
  107.3 5.2 %copy-start.1 = (bf16[256,512]{1,0:T(8,128)(2,1)S(1)}, bf16[256,512]{1,0:T(8,128)(2,1)}, u32[]{:S(2)}) copy-start(bf16[256,512]{1,0:T(8,128)(2,1)} %get-tuple-element.16) | copy-start | bytes 786436
  107.4 5.9 %copy-start = (bf16[256,512]{1,0:T(8,128)(2,1)S(1)}, bf16[256,512]{1,0:T(8,128)(2,1)}, u32[]{:S(2)}) copy-start(bf16[256,512]{1,0:T(8,128)(2,1)} %get-tuple-element.17) | copy-start | bytes 786436
  107.4 6.6 %copy-start.2 = (f32[1,512]{1,0:T(1,128)S(1)}, f32[1,512]{1,0:T(1,128)}, u32[]{:S(2)}) copy-start(f32[1,512]{1,0:T(1,128)} %get-tuple-element.11) | copy-start | bytes 6148

commit v4 on v3

--- a/solution.py
+++ b/solution.py
@@ -410,35 +410,34 @@
         at_distance(distance, forward)
         advance_if(4)
 
-    pending = list(range(1, nb - 1))
-    for h in range(HEADS):
-        part = slice(h * HEAD_DIM, (h + 1) * HEAD_DIM)
-        kh, vh, ga = k_t[part, :], v_t[part, :], ga_t[part, :]
-        inv = 1.0 / den[h : h + 1, :]
-        attn = (num[part, :] * inv).astype(BF16)
-        attn_t[part, :] = attn
-        correction = jnp.sum(ga * attn.astype(F32), axis=0, keepdims=True) * inv
-        stats[h : h + 1, :] = inv
-        stats[HEADS + h : HEADS + h + 1, :] = correction
-        dots = mul(vh, (ga * inv).astype(BF16), 0, 0)
-        slopes = (w_all[h].astype(F32) * (dots - correction)).astype(BF16)
-        dq_f[part, :] = mul(kh, slopes, 1, 0) * SCALE
-        if h % 2 == 1:
-            advance_if(4)
-        if h % 3 == 2 and pending:
-            step = pending.pop(0)
-            line_recv(step - 1, (1,))
-            line_send(step, (1,))
-    for step in pending:
-        line_recv(step - 1, (1,))
-        line_send(step, (1,))
+    inv = 1.0 / den[...]
+    ga_heads = ga_t[...].reshape(HEADS, HEAD_DIM, rows)
+    attn = (num[...].reshape(HEADS, HEAD_DIM, rows) * inv[:, None, :]).astype(BF16)
+    correction = jnp.sum(ga_heads * attn.astype(F32), axis=1) * inv
+    attn_t[...] = attn.reshape(width, rows)
+    gh_t[...] = (ga_heads * inv[:, None, :]).reshape(width, rows).astype(BF16)
+    stats[:HEADS, :] = inv
+    stats[HEADS:, :] = correction
     for k in range(1, nb):
         to = lax.rem(me + k, nb)
         remote(stats, all_stats.at[me], ssend.at[k], srecv.at[k], "blk", to).start()
     all_stats[me] = stats[...]
-    dq = head_norm_pull(queries, q_scaling, dq_f[...]).astype(BF16)
     terms[3] = mul(attn_t[...], gout[...], 1, 0).astype(BF16)
     begin(3)
+
+    for h in range(HEADS):
+        part = slice(h * HEAD_DIM, (h + 1) * HEAD_DIM)
+        dots = mul(v_t[part, :], gh_t[part, :], 0, 0)
+        slopes = (w_all[h].astype(F32) * (dots - stats[HEADS + h : HEADS + h + 1, :])).astype(BF16)
+        dq_f[part, :] = mul(k_t[part, :], slopes, 1, 0) * SCALE
+        if h == 5:
+            for step in range(1, min(2, nb - 1)):
+                line_recv(step - 1, (1,))
+                line_send(step, (1,))
+        if h % 4 == 3:
+            advance_if(4)
+            advance_if(3)
+    dq = head_norm_pull(queries, q_scaling, dq_f[...]).astype(BF16)
     terms[0] = mul(normed, dq, 0, 1).astype(BF16)
     begin(0)
     out = x + mul(mean_rows[...], wm[...], 1, 0) + mul(attn_t[...], wo[...], 0, 0)
@@ -480,6 +479,9 @@
         origin = lax.rem(me + nb - k, nb)
         remote(stats, all_stats.at[origin], ssend.at[k], srecv.at[k], "blk", to).wait()
     for distance in range(1, nb - 1):
+        if distance > 1:
+            line_recv(distance - 1, (1,))
+            line_send(distance, (1,))
         at_distance(distance, backward)
         for p in (4, 3, 0):
             advance_if(p)

time: 115 us -> 111 us (0.965)
  Pallas kernels: 112 us -> 108 us
    pallas_call x1, Pallas kernels: 107 us -> 103 us  [layer_call(): pl.pallas_call(partial(layer_kernel, nd, nb), out_shape=[jax.ShapeDtypeSt...]
where the time goes in v4:
time: 111 us
  Pallas kernels  108 us (97%)
  local copies, waits for them, and re-layouts  2 us (2%)
    pallas_call x1, Pallas kernels, layer_call(): pl.pallas_call(partial(layer_kernel, nd, nb), out_shape=[jax.ShapeDtypeSt...  103 us
    pallas_call x1, Pallas kernels, widen(): pl.pallas_call(widen_kernel, grid=(PIECES,), out_shape=jax.ShapeDtypeStru...  5.2 us

profile of v4, /device:TPU:0, one launch (start us, length us, event | category | flops | bytes accessed | tf_op | source)
XLA Modules:
  0.0 110.6 jit_solution(4894508434987142889)
XLA Ops:
  0.6 102.7 %shard_map.165 = (bf16[256,512]{1,0:T(8,128)(2,1)}, bf16[256,512]{1,0:T(8,128)(2,1)}, bf16[2560,512]{1,0:T(8,128)(2,1)}, f32[1,512]{1,0:T(1,128)}) custom-call(bf16[256,512]{1,0:T(8,128)(2,1)} %feat.1, bf16[256,512]{1,0:T(8,128)(2,1)} %gout.1, f32[1,512]{1,0:T(1,128)} %bitcast.7, bf16[512,512]{1,0:T(8,128)(2,1)} %wq.1, bf16[512,512]{1,0:T(8,128)(2,1)} %wk.1, ...), custom_call_target="tpu_custom_call" | custom-call | tf_op jit(solution)/shard_map/pallas_call | solution.py:540
  103.4 0.0 copy-start.1
  103.4 0.0 copy-start
  103.4 0.0 copy-start.2
  103.4 5.2 %shard_map.166 = f32[5,512,512]{2,1,0:T(8,128)} custom-call(bf16[2560,512]{1,0:T(8,128)(2,1)} %get-tuple-element.10.x), custom_call_target="tpu_custom_call" | custom-call | tf_op jit(solution)/shard_map/pallas_call | solution.py:586
  108.6 0.0 copy-done.1
  108.6 0.7 copy.21
  109.3 0.0 copy-done
  109.3 0.7 copy.22
  110.0 0.0 copy-done.2
  110.0 0.6 copy.23
Async XLA Ops:
  103.4 5.2 %copy-start.1 = (bf16[256,512]{1,0:T(8,128)(2,1)S(1)}, bf16[256,512]{1,0:T(8,128)(2,1)}, u32[]{:S(2)}) copy-start(bf16[256,512]{1,0:T(8,128)(2,1)} %get-tuple-element.16) | copy-start | bytes 786436
  103.4 5.9 %copy-start = (bf16[256,512]{1,0:T(8,128)(2,1)S(1)}, bf16[256,512]{1,0:T(8,128)(2,1)}, u32[]{:S(2)}) copy-start(bf16[256,512]{1,0:T(8,128)(2,1)} %get-tuple-element.17) | copy-start | bytes 786436
  103.4 6.6 %copy-start.2 = (f32[1,512]{1,0:T(1,128)S(1)}, f32[1,512]{1,0:T(1,128)}, u32[]{:S(2)}) copy-start(f32[1,512]{1,0:T(1,128)} %get-tuple-element.11) | copy-start | bytes 6148
